TPU v7x, 32 devices: a whole 2x2x4 slice. The times are simulated.
32 devices in a mesh: rows: 8 (over z, x), cls: 4 (over y, core).
Axes of the slice: x: 2, y: 2, z: 4, core: 2. Of those that a mesh axis runs over, the one named last changes fastest.
Arguments:
- centers: bfloat16 [2048, 1280], P('rows', 'cls'), may hold values from 0 to 4
- coefficients: float32 [1000, 2048], P('cls', 'rows'), may hold values from -0.6 to 0.6
- batch_features: bfloat16 [1024, 1280], P('rows', 'cls'), may hold values from 0 to 4
- batch_labels: int32 [1024], replicated, may hold values from 0 to 999
- batch_index: int32 [1024], replicated, may hold values from 0 to 2047
- subset_index: int32 [512], P('rows'), may hold values from 0 to 2047, as said below
- eigen_vectors: float32 [512, 512], P('rows'), may hold values from -0.25 to 0.25
- eigen_scale: float32 [512], replicated, may hold values from 0.2 to 2
Outputs:
- predicted: float32 [1000, 1024], P('cls')
- new_coefficients: float32 [1000, 2048], P('cls', 'rows')
Inputs may be any that keep to these rules, and one draw needn't show every extreme that they name: `subset_index`: entry s lies among the centers (s // 64) * 256 to (s // 64 + 1) * 256 - 1; entry 0 is 0 and the last is 2047.
All inputs are finite; a program needn't handle non-finite values.
Results may differ from a plain program's by a relative error of at most 0.0003.
Values may be sent and summed in bfloat16 or wider, within the bound.
A program may use at most 64 MiB of HBM per device.

v0:
```python
import jax
import jax.numpy as jnp
from jax import lax
from jax.sharding import PartitionSpec as P

spread = 4.0
step_rate = 0.5


def kernel_block(inner, row_norm, col_norm):
    squared = row_norm[:, None] + col_norm[None, :] - 2.0 * inner
    return jnp.exp(-jnp.sqrt(jnp.maximum(squared, 0.0)) / spread)


def square_norm(features):
    return jnp.sum(jnp.square(features.astype(jnp.float32)), axis=1)


def shards(
    centers,
    coefficients,
    batch_features,
    batch_labels,
    batch_index,
    subset_index,
    eigen_vectors,
    eigen_scale,
):
    row_count = centers.shape[0]
    first_row = lax.axis_index("rows") * row_count
    subset_local = subset_index - first_row
    subset_rows = centers[subset_local]
    batch_rows = lax.all_gather(batch_features, "rows", axis=0, tiled=True)
    batch_whole = lax.all_gather(batch_rows, "cls", axis=1, tiled=True)
    batch_norm = square_norm(batch_whole)
    pieces = (
        lax.all_gather(centers, "cls", axis=1, tiled=True),
        lax.all_gather(subset_rows, "cls", axis=1, tiled=True),
    )
    center_inner = jnp.einsum(
        "cd,bd->cb", pieces[0], batch_whole, preferred_element_type=jnp.float32
    )
    center_norm = square_norm(pieces[0])
    subset_inner = jnp.einsum(
        "cd,bd->cb", pieces[1], batch_whole, preferred_element_type=jnp.float32
    )
    subset_norm = square_norm(pieces[1])
    center_inner, center_norm, subset_inner, subset_norm = (
        center_inner,
        center_norm,
        subset_inner,
        subset_norm,
    )
    kernel_centers = kernel_block(center_inner, center_norm, batch_norm)
    subset_kernel = kernel_block(subset_inner, subset_norm, batch_norm)
    partial_pred = jnp.dot(coefficients, kernel_centers, precision=lax.Precision.HIGHEST)
    class_count = coefficients.shape[0]
    class_start = lax.axis_index("cls") * class_count
    class_ids = jnp.arange(class_count, dtype=jnp.int32) + class_start
    targets = (batch_labels[None, :] == class_ids[:, None]).astype(jnp.float32)
    basis_part = jnp.dot(eigen_vectors.T, subset_kernel, precision=lax.Precision.HIGHEST)
    predicted, basis_sum = lax.psum((partial_pred, basis_part), "rows")
    gradient = predicted - targets
    projected = jnp.dot(gradient, basis_sum.T, precision=lax.Precision.HIGHEST)
    correction = jnp.dot(
        projected * eigen_scale[None, :], eigen_vectors.T, precision=lax.Precision.HIGHEST
    )
    batch_local = batch_index - first_row
    is_owned = (batch_local >= 0) & (batch_local < row_count)
    batch_slot = jnp.where(is_owned, batch_local, row_count)
    updated = coefficients.at[:, batch_slot].add(-step_rate * gradient, mode="drop")
    updated = updated.at[:, subset_local].add(step_rate * correction)
    return (predicted, updated)


def solution(mesh):
    return jax.shard_map(
        shards,
        mesh=mesh,
        in_specs=(
            P("rows", "cls"),
            P("cls", "rows"),
            P("rows", "cls"),
            P(),
            P(),
            P("rows"),
            P("rows", None),
            P(),
        ),
        out_specs=(P("cls", None), P("cls", "rows")),
        check_vma=False,
    )
```

profile of v0, /device:TPU:0, one launch (start us, length us, event | category | flops | bytes accessed | tf_op | source)
XLA Modules:
  0.0 229.4 jit_solution(11725823975673172979)
XLA Ops:
  7.2 0.0 copy-start
  7.2 0.0 copy-start.4
  7.2 0.0 all-gather.4.cloned.1.call-start
  7.2 31.9 %all_gather.13 = bf16[1024,320]{0,1:T(8,128)(2,1)} all-gather(bf16[128,320]{0,1:T(8,128)(2,1)} %param.10), channel_id=1, replica_groups=mesh['rows'=8,'cls'=4] {'rows'}, dimensions={0}, use_global_device_ids=true | all-gather | bytes 737280 | tf_op jit(solution)/shard_map/all_gather | solution.py:33
  39.1 0.0 all-gather.4.cloned.1.call-update
  39.2 0.0 all-reduce.3.cloned.1.call-start
  39.2 1.1 copy.20
  40.3 0.7 compare_select_fusion.1
  41.0 0.7 gather_fusion
  41.7 5.6 %all-gather.1 = bf16[4,320,64]{1,2,0:T(8,128)(2,1)S(1)} all-gather(bf16[1,320,64]{1,2,0:T(8,128)(2,1)S(1)} %bitcast.25), channel_id=2, replica_groups=mesh['rows'=8,'cls'=4] {'cls'}, dimensions={0}, use_global_device_ids=true | all-gather | bytes 204800 | tf_op jit(solution)/shard_map/all_gather | solution.py:38
  47.3 0.2 copy.21
  47.5 0.2 reshape.42
  47.6 0.1 multiply_reduce_fusion.2
  47.8 0.0 copy-done.4
  47.8 12.2 %all_gather.12 = bf16[256,1280]{0,1:T(8,128)(2,1)S(1)} all-gather(bf16[256,320]{0,1:T(8,128)(2,1)S(1)} %copy-done.4), channel_id=1, replica_groups=mesh['rows'=8,'cls'=4] {'cls'}, dimensions={1}, use_global_device_ids=true | all-gather | bytes 819200 | tf_op jit(solution)/shard_map/all_gather | solution.py:37
  59.9 0.2 multiply_reduce_fusion.1
  60.1 6.5 %all-gather.4.cloned.1.call-done = bf16[1024,1280]{0,1:T(8,128)(2,1)} async-done(((bf16[1024,320]{0,1:T(8,128)(2,1)}), bf16[1024,1280]{0,1:T(8,128)(2,1)}) %all-gather.4.cloned.1.call-update) | async-done | bytes 2621456 | tf_op jit(solution)/shard_map/all_gather | solution.py:34
  66.6 0.0 copy-start.1
  66.6 2.5 %multiply_reduce_fusion = f32[1024]{0:T(1024)S(1)} fusion(bf16[1024,1280]{0,1:T(8,128)(2,1)} %all-gather.4.cloned.1.call-done), kind=kLoop, calls=%fused_computation.3 | loop fusion | flops 3931136 | bytes 2625536 | tf_op jit(solution)/shard_map/reduce_sum | solution.py:16
  69.1 0.0 copy-done.1
  69.2 0.0 copy-start.3
  69.2 1.2 fusion.5
  70.4 0.0 copy-done.3
  70.4 2.8 %convolution_bitcast_fusion.1 = f32[250,1024]{0,1:T(8,128)} fusion(f32[256,1024]{1,0:T(8,128)S(1)} %fusion.5, f32[250,256]{1,0:T(8,128)S(1)} %copy-done.3), kind=kOutput, calls=%fused_computation.5 | convolution fusion | flops 786432000 | bytes 2328576 | tf_op jit(solution)/shard_map/dot_general | solution.py:56
  73.2 0.7 fusion.11
  73.9 0.0 copy-done
  73.9 0.0 copy-start.6
  73.9 3.1 %convolution_bitcast_fusion = f32[512,1024]{0,1:T(8,128)} fusion(f32[64,1024]{1,0:T(8,128)S(1)} %fusion.11, f32[64,512]{1,0:T(8,128)S(1)} %copy-done), kind=kOutput, calls=%fused_computation.4 | convolution fusion | flops 402653184 | bytes 2490368 | tf_op jit(solution)/shard_map/dot_general | solution.py:61
  77.0 0.0 copy-start.5
  77.0 0.0 copy-start.7
  77.0 0.0 all-reduce.3.cloned.1.call-update
  77.0 0.1 copy.19
  77.2 0.0 copy-done.6
  77.2 129.5 %all-reduce.3.cloned.1.call-done = (f32[250,1024]{0,1:T(8,128)}, f32[512,1024]{0,1:T(8,128)}) async-done(((f32[250,1024]{0,1:T(8,128)}, f32[512,1024]{0,1:T(8,128)}), (f32[250,1024]{0,1:T(8,128)}, f32[512,1024]{0,1:T(8,128)})) %all-reduce.3.cloned.1.call-update) | async-done | bytes 3121168 | tf_op jit(solution)/shard_map/psum | solution.py:62
  206.7 0.0 copy-start.2
  206.7 2.6 %copy.22 = f32[250,1024]{1,0:T(8,128)} copy(f32[250,1024]{0,1:T(8,128)} %get-tuple-element.8) | data formatting | bytes 2048000
  209.3 0.0 copy-done.5
  209.3 0.0 copy-done.7
  209.3 0.0 copy-done.2
  209.3 3.8 %convolution_multiply_fusion.1 = f32[250,512]{1,0:T(8,128)S(1)} fusion(f32[512,1024]{0,1:T(8,128)} %get-tuple-element.9, f32[250,1024]{0,1:T(8,128)S(1)} %copy-done.2, s32[250]{0:T(256)S(1)} %iota_add_fusion, s32[1024]{0:T(1024)S(1)} %copy-done.5, f32[512]{0:T(512)S(1)} %copy-done.7), kind=kOutput, calls=%fused_computation.14 | convolution fusion | flops 1573760000 | bytes 3640296 | tf_op jit(solution)/shard_map/dot_general | solution.py:64
  213.2 0.6 fusion.12
  213.8 6.9 %scatter_custom_fusion = f32[250,256]{0,1:T(8,128)S(1)} fusion(f32[250,256]{0,1:T(8,128)S(1)} %copy.19, s32[1024]{0:T(1024)S(1)} %compare_select_fusion, f32[250,1024]{0,1:T(8,128)S(1)} %copy-done.2, f32[]{:T(128)} %constant.7.clone.1, s32[250]{0:T(256)S(1)} %iota_add_fusion, s32[1024]{0:T(1024)S(1)} %copy-done.5), kind=kCustom, calls=%fused_computation.24 | custom fusion | flops 1280000 | bytes 1309700 | tf_op jit(solution)/shard_map/scatter-add | solution.py:71
  220.7 1.1 scatter_fusion
  221.7 0.8 copy.23
  (3 shorter events, 0.0 us)
Async XLA Ops:
  7.2 66.7 %copy-start = (f32[64,512]{1,0:T(8,128)S(1)}, f32[64,512]{1,0:T(8,128)}, u32[]{:S(2)}) copy-start(f32[64,512]{1,0:T(8,128)} %param.14) | copy-start | bytes 393220
  7.2 40.6 %copy-start.4 = (bf16[256,320]{0,1:T(8,128)(2,1)S(1)}, bf16[256,320]{0,1:T(8,128)(2,1)}, u32[]{:S(2)}) copy-start(bf16[256,320]{0,1:T(8,128)(2,1)} %param.8) | copy-start | bytes 491524
  7.2 59.4 %all-gather.4.cloned.1.call-start = ((), (), s32[]{:S(2)}) async-start(), calls=%async_computation | async-start | bytes 3276800 | tf_op jit(solution)/shard_map/all_gather | solution.py:34
  39.2 167.5 %all-reduce.3.cloned.1.call-start = ((), (), s32[]{:S(2)}) async-start(), calls=%async_computation.1 | async-start | bytes 6291456 | tf_op jit(solution)/shard_map/psum | solution.py:62
  66.6 2.5 %copy-start.1 = (bf16[1024,1280]{0,1:T(8,128)(2,1)S(1)}, bf16[1024,1280]{0,1:T(8,128)(2,1)}, u32[]{:S(2)}) copy-start(bf16[1024,1280]{0,1:T(8,128)(2,1)} %all-gather.4.cloned.1.call-done) | copy-start | bytes 7864324
  69.2 1.2 copy-start.3
  73.9 3.3 %copy-start.6 = (s32[1024]{0:T(1024)S(1)}, s32[1024]{0:T(1024)}, u32[]{:S(2)}) copy-start(s32[1024]{0:T(1024)} %param.12) | copy-start | bytes 12292
  77.0 132.3 %copy-start.5 = (s32[1024]{0:T(1024)S(1)}, s32[1024]{0:T(1024)}, u32[]{:S(2)}) copy-start(s32[1024]{0:T(1024)} %param.11) | copy-start | bytes 12292
  77.0 132.3 %copy-start.7 = (f32[512]{0:T(512)S(1)}, f32[512]{0:T(512)}, u32[]{:S(2)}) copy-start(f32[512]{0:T(512)} %param.15) | copy-start | bytes 6148
  206.7 2.6 %copy-start.2 = (f32[250,1024]{0,1:T(8,128)S(1)}, f32[250,1024]{0,1:T(8,128)}, u32[]{:S(2)}) copy-start(f32[250,1024]{0,1:T(8,128)} %get-tuple-element.8) | copy-start | bytes 3072004
Sparse Core Ops, SparseCore 0:
  39.3 27.2 all-gather.3
  77.2 129.4 all-reduce.2
where the time goes:
time: 230 us; the launch traced here: 229 us
  waiting for transfers between devices  136 us (59%)
  blocking collectives  49.7 us (22%)
  between operations  14.2 us (6%)
  matrix products  12.2 us (5%)
  other arithmetic  11.5 us (5%)
  local copies, waits for them, and re-layouts  5.77 us (3%)
    psum x1, waiting for transfers between devices, shards(): predicted, basis_sum = lax.psum((partial_pred, basis_part), 'rows')  129 us
    all_gather x1, blocking collectives, shards(): batch_rows = lax.all_gather(batch_features, 'rows', axis=0, tiled=True)  31.9 us
    all_gather x1, blocking collectives, shards(): lax.all_gather(centers, 'cls', axis=1, tiled=True)  12.2 us
    scatter-add x1, other arithmetic, shards(): coefficients.at[:, batch_slot].add(-step_rate * gradient, mode='drop')  6.89 us
    all_gather x1, waiting for transfers between devices, shards(): batch_whole = lax.all_gather(batch_rows, 'cls', axis=1, tiled=True)  6.52 us
    all_gather x1, blocking collectives, shards(): lax.all_gather(subset_rows, 'cls', axis=1, tiled=True)  5.6 us
    unnamed x21, local copies, waits for them, and re-layouts  4.91 us
  transfers between devices with their start and end apart: 2, of which 2 were waited for; matrix products, arithmetic and copies ran while one was open for 1% of the time, Pallas kernels for 0%

commit v1 on v0

v1 whole, which is shorter than its diff:
```python
import functools

import jax
import jax.numpy as jnp
from jax import lax
from jax.experimental import pallas as pl
from jax.experimental.pallas import tpu as pltpu
from jax.sharding import PartitionSpec as P

spread = 4.0
step_rate = 0.5
HIGHEST = lax.Precision.HIGHEST
MESH = pl.DeviceIdType.MESH
NX = 2
NCORE = 2


def kernel_block(inner, row_norm, col_norm):
    squared = row_norm + col_norm - 2.0 * inner
    return jnp.exp(-jnp.sqrt(jnp.maximum(squared, 0.0)) / spread)


def square_norm(features):
    return jnp.sum(jnp.square(features.astype(jnp.float32)), axis=1)


def dot_nt(a, b, precision=None):
    return lax.dot_general(
        a, b, (((1,), (1,)), ((), ())),
        preferred_element_type=jnp.float32, precision=precision,
    )


def dot_tn(a, b, precision=None):
    return lax.dot_general(
        a, b, (((0,), (0,)), ((), ())),
        preferred_element_type=jnp.float32, precision=precision,
    )


def dot_nn(a, b, precision=None):
    return jnp.dot(a, b, preferred_element_type=jnp.float32, precision=precision)


def fused_kernel(
    rows, cls, class_count,
    cen_ref, coef_ref, bat_ref, lab_ref, idx_ref, sub_ref, eig_ref, scale_ref,
    pred_ref, new_ref,
    batch, cen, eig, coefp, sk, xsend, acc, xrecv, zrecv, pred, eall, gmat, upd,
    send_sem, recv_sem, xs_send, xs_recv,
):
    nz = rows // NX
    r = lax.axis_index("rows")
    c = lax.axis_index("cls")
    z, x = r // NX, r % NX
    y, k = c // NCORE, c % NCORE
    rx = z * NX + (1 - x)
    cy = (1 - y) * NCORE + k
    ck = y * NCORE + (1 - k)
    cyk = (1 - y) * NCORE + (1 - k)
    row_count = cen_ref.shape[0]
    cols = bat_ref.shape[0]
    subset_count = eig_ref.shape[0]
    eig_part = subset_count // cls
    first_row = r * row_count

    def zrow(d):
        return lax.rem(z + d, nz) * NX + x

    def zback(d):
        return lax.rem(z + nz - d, nz) * NX + x

    x_dev = (rx, c)
    y_dev = (r, cy)
    k_dev = (r, ck)

    def z_dev(d):
        return (zrow(d), c)

    barrier = pltpu.get_barrier_semaphore()
    partners = [x_dev, y_dev, k_dev] + [z_dev(d) for d in range(1, nz)]
    for dev in partners:
        pl.semaphore_signal(barrier, inc=1, device_id=dev, device_id_type=MESH)
    pl.semaphore_wait(barrier, len(partners))

    sent = []
    count = [0]

    def send(src, dst, dev):
        n = count[0]
        count[0] += 1
        copy = pltpu.make_async_remote_copy(
            src_ref=src, dst_ref=dst, send_sem=send_sem.at[n], recv_sem=recv_sem.at[n],
            device_id=dev, device_id_type=MESH,
        )
        copy.start()
        sent.append(copy)

        def arrive(slot):
            pltpu.make_async_remote_copy(
                src_ref=slot, dst_ref=slot, send_sem=send_sem.at[n], recv_sem=recv_sem.at[n],
                device_id=dev, device_id_type=MESH,
            ).wait_recv()

        return arrive

    core_waits = []
    pairs = [(r, c)]

    def to_core(src, row, col, other):
        core_waits.append((send(src, batch.at[row, col], k_dev), row, other))

    own = bat_ref
    z_waits = [send(own, batch.at[r, c], z_dev(d)) for d in range(1, nz)]
    y_waits = [(send(own, batch.at[r, c], y_dev), r)]
    x_waits = [(send(own, batch.at[r, c], x_dev), rx, c)]
    cen_k = send(cen_ref, cen.at[c], k_dev)
    cen_y = send(cen_ref, cen.at[c], y_dev)
    to_core(own, r, c, ck)
    eig_own = eig_ref.at[pl.ds(pl.multiple_of(c * eig_part, eig_part), eig_part)]
    batch[r, c] = bat_ref[...]
    cen[c] = cen_ref[...]
    eig[r, c] = eig_ref[pl.ds(pl.multiple_of(c * eig_part, eig_part), eig_part), :]
    coefp[...] = jnp.zeros_like(coefp)
    coefp[pl.ds(0, class_count), :] = coef_ref[...]
    for d in range(1, nz):
        row = zback(d)
        z_waits[d - 1](batch.at[row, c])
        y_waits.append((send(batch.at[row, c], batch.at[row, c], y_dev), row))
        x_waits.append((send(batch.at[row, c], batch.at[row, c], x_dev), row + 1 - 2 * x, c))
        to_core(batch.at[row, c], row, c, ck)
    cen_y(cen.at[cy])
    cen_yk = send(cen.at[cy], cen.at[cy], k_dev)
    for arrive, row in y_waits:
        arrive(batch.at[row, cy])
        x_waits.append((send(batch.at[row, cy], batch.at[row, cy], x_dev), row + 1 - 2 * x, cy))
        to_core(batch.at[row, cy], row, cy, cyk)
    ez_waits = [send(eig_own, eig.at[r, c], z_dev(d)) for d in range(1, nz)]
    for arrive, row, col in x_waits:
        arrive(batch.at[row, col])
        send_to = cyk if col is cy else ck
        to_core(batch.at[row, col], row, col, send_to)
    cen_k(cen.at[ck])
    cen_yk(cen.at[cyk])
    for arrive, row, col in core_waits:
        arrive(batch.at[row, col])

    ex_waits = [(send(eig_own, eig.at[r, c], x_dev), rx)]
    for d in range(1, nz):
        row = zback(d)
        ez_waits[d - 1](eig.at[row, c])
        ex_waits.append((send(eig.at[row, c], eig.at[row, c], x_dev), row + 1 - 2 * x))

    cen_norm = jnp.zeros((row_count, 1), jnp.float32)
    for q in range(cls):
        part = cen[q].astype(jnp.float32)
        cen_norm += jnp.sum(part * part, axis=1, keepdims=True)
    subset_local = sub_ref[...] - first_row
    pick = (
        lax.broadcasted_iota(jnp.int32, (row_count, subset_count), 0) == subset_local
    ).astype(jnp.float32)
    ones = jnp.ones((16, bat_ref.shape[1]), jnp.bfloat16)

    def part_pred(row):
        inner = jnp.zeros((row_count, cols), jnp.float32)
        norm = jnp.zeros((16, cols), jnp.float32)
        for q in range(cls):
            block = batch[row, q]
            inner += dot_nt(cen[q], block)
            wide = block.astype(jnp.float32)
            square = wide * wide
            high = square.astype(jnp.bfloat16)
            low = (square - high.astype(jnp.float32)).astype(jnp.bfloat16)
            norm += dot_nt(ones, high) + dot_nt(ones, low)
        kern = kernel_block(inner, cen_norm, norm[0:1, :])
        sk[row] = dot_tn(pick, kern, HIGHEST)
        return dot_nn(coefp[...], kern, HIGHEST)

    def x_copy(zz):
        return pltpu.make_async_remote_copy(
            src_ref=xsend.at[zz], dst_ref=xrecv.at[zz],
            send_sem=xs_send.at[zz], recv_sem=xs_recv.at[zz],
            device_id=x_dev, device_id_type=MESH,
        )

    def peer_chunk(zz, carry):
        xsend[zz] = part_pred(zz * NX + (1 - x))
        x_copy(zz).start()
        return carry

    def own_chunk(zz, carry):
        acc[zz] = part_pred(zz * NX + x)
        return carry

    lax.fori_loop(0, nz, peer_chunk, 0)
    lax.fori_loop(0, nz, own_chunk, 0)

    rs_waits = []
    for d in range(1, nz):
        zz = lax.rem(z + d, nz)
        x_copy(zz).wait()
        acc[zz] += xrecv[zz]
        rs_waits.append(send(acc.at[zz], zrecv.at[d - 1], z_dev(d)))
    x_copy(z).wait()
    total = acc[z] + xrecv[z]

    ey_waits, ek_waits = [], []
    ey_waits.append((send(eig_own, eig.at[r, c], y_dev), r))
    ek_waits.append((send(eig_own, eig.at[r, c], k_dev), r, ck))
    for d in range(1, nz):
        row = zback(d)
        ey_waits.append((send(eig.at[row, c], eig.at[row, c], y_dev), row))
        ek_waits.append((send(eig.at[row, c], eig.at[row, c], k_dev), row, ck))
    for arrive, row in ex_waits:
        arrive(eig.at[row, c])
        ey_waits.append((send(eig.at[row, c], eig.at[row, c], y_dev), row))
        ek_waits.append((send(eig.at[row, c], eig.at[row, c], k_dev), row, ck))

    for d in range(1, nz):
        rs_waits[d - 1](zrecv.at[d - 1])
        total += zrecv[d - 1]
    pred[r] = total

    ag_waits = [send(pred.at[r], pred.at[r], z_dev(d)) for d in range(1, nz)]
    ax_waits = [(send(pred.at[r], pred.at[r], x_dev), rx)]

    for arrive, row in ey_waits:
        arrive(eig.at[row, cy])
        ek_waits.append((send(eig.at[row, cy], eig.at[row, cy], k_dev), row, cyk))

    class_ids = lax.broadcasted_iota(jnp.int32, (coefp.shape[0], cols), 0) + c * class_count
    center_ids = lax.broadcasted_iota(jnp.int32, (row_count, cols), 0) + first_row

    def use_chunk(row, et):
        value = pred[row]
        pred_ref[:, pl.ds(pl.multiple_of(row * cols, cols), cols)] = value[0:class_count]
        grad = value - (lab_ref[pl.ds(row, 1), :] == class_ids).astype(jnp.float32)
        hit = (idx_ref[pl.ds(row, 1), :] == center_ids).astype(jnp.float32)
        upd[...] += dot_nt(grad, hit, HIGHEST)
        return et + dot_nt(sk[row], grad, HIGHEST)

    upd[...] = jnp.zeros_like(upd)
    et = use_chunk(r, jnp.zeros((subset_count, coefp.shape[0]), jnp.float32))
    for d in range(1, nz):
        row = zback(d)
        ag_waits[d - 1](pred.at[row])
        ax_waits.append((send(pred.at[row], pred.at[row], x_dev), row + 1 - 2 * x))
        et = use_chunk(row, et)
    for arrive, row, col in ek_waits:
        arrive(eig.at[row, col])
    whole = eig[...].reshape(rows * subset_count, eig_ref.shape[1])
    gmat[...] = dot_nt(eig_ref[...] * scale_ref[...], whole, HIGHEST)
    for arrive, row in ax_waits:
        arrive(pred.at[row])
        et = use_chunk(row, et)

    eall[r] = et
    fz_waits = [send(eall.at[r], eall.at[r], z_dev(d)) for d in range(1, nz)]
    fx_waits = [(send(eall.at[r], eall.at[r], x_dev), rx)]
    for d in range(1, nz):
        row = zback(d)
        fz_waits[d - 1](eall.at[row])
        fx_waits.append((send(eall.at[row], eall.at[row], x_dev), row + 1 - 2 * x))
    for arrive, row in fx_waits:
        arrive(eall.at[row])
    errors = eall[...].reshape(rows * subset_count, coefp.shape[0])
    correction = dot_nn(gmat[...], errors, HIGHEST)
    moved = dot_tn(correction, jnp.transpose(pick), HIGHEST)
    result = coefp[...] - step_rate * upd[...] + step_rate * moved
    new_ref[...] = result[0:class_count]
    for copy in sent:
        copy.wait_send()


def fused_shards(
    rows, cls,
    centers, coefficients, batch_features, batch_labels, batch_index,
    subset_index, eigen_vectors, eigen_scale,
):
    row_count, width = centers.shape
    class_count = coefficients.shape[0]
    cols = batch_features.shape[0]
    subset_count, eig_count = eigen_vectors.shape
    padded = -(-class_count // 8) * 8
    nz = rows // NX
    copies = 200
    f32 = jnp.float32
    vmem = pl.BlockSpec(memory_space=pltpu.VMEM)
    return pl.pallas_call(
        functools.partial(fused_kernel, rows, cls, class_count),
        out_shape=(
            jax.ShapeDtypeStruct((class_count, rows * cols), f32),
            jax.ShapeDtypeStruct((class_count, row_count), f32),
        ),
        in_specs=[vmem] * 8,
        out_specs=(vmem, vmem),
        scratch_shapes=[
            pltpu.VMEM((rows, cls, cols, width), jnp.bfloat16),
            pltpu.VMEM((cls, row_count, width), jnp.bfloat16),
            pltpu.VMEM((rows, cls, subset_count // cls, eig_count), f32),
            pltpu.VMEM((padded, row_count), f32),
            pltpu.VMEM((rows, subset_count, cols), f32),
            pltpu.VMEM((nz, padded, cols), f32),
            pltpu.VMEM((nz, padded, cols), f32),
            pltpu.VMEM((nz, padded, cols), f32),
            pltpu.VMEM((nz - 1, padded, cols), f32),
            pltpu.VMEM((rows, padded, cols), f32),
            pltpu.VMEM((rows, subset_count, padded), f32),
            pltpu.VMEM((subset_count, rows * subset_count), f32),
            pltpu.VMEM((padded, row_count), f32),
            pltpu.SemaphoreType.DMA((copies,)),
            pltpu.SemaphoreType.DMA((copies,)),
            pltpu.SemaphoreType.DMA((nz,)),
            pltpu.SemaphoreType.DMA((nz,)),
        ],
        compiler_params=pltpu.CompilerParams(
            collective_id=0, has_side_effects=True, vmem_limit_bytes=48 * 1024 * 1024
        ),
    )(
        centers, coefficients, batch_features,
        batch_labels.reshape(rows, cols), batch_index.reshape(rows, cols),
        subset_index.reshape(1, subset_count), eigen_vectors,
        eigen_scale.reshape(1, eig_count),
    )


def plain_shards(
    centers, coefficients, batch_features, batch_labels, batch_index,
    subset_index, eigen_vectors, eigen_scale,
):
    row_count = centers.shape[0]
    first_row = lax.axis_index("rows") * row_count
    subset_local = subset_index - first_row
    batch_rows = lax.all_gather(batch_features, "rows", axis=0, tiled=True)
    batch_whole = lax.all_gather(batch_rows, "cls", axis=1, tiled=True)
    batch_norm = square_norm(batch_whole)
    center_whole = lax.all_gather(centers, "cls", axis=1, tiled=True)
    inner = jnp.einsum("cd,bd->cb", center_whole, batch_whole, preferred_element_type=jnp.float32)
    kernel_centers = kernel_block(
        inner, square_norm(center_whole)[:, None], batch_norm[None, :]
    )
    subset_kernel = kernel_centers[subset_local]
    partial_pred = jnp.dot(coefficients, kernel_centers, precision=HIGHEST)
    class_count = coefficients.shape[0]
    class_start = lax.axis_index("cls") * class_count
    class_ids = jnp.arange(class_count, dtype=jnp.int32) + class_start
    targets = (batch_labels[None, :] == class_ids[:, None]).astype(jnp.float32)
    basis_part = jnp.dot(eigen_vectors.T, subset_kernel, precision=HIGHEST)
    predicted, basis_sum = lax.psum((partial_pred, basis_part), "rows")
    gradient = predicted - targets
    projected = jnp.dot(gradient, basis_sum.T, precision=HIGHEST)
    correction = jnp.dot(
        projected * eigen_scale[None, :], eigen_vectors.T, precision=HIGHEST
    )
    batch_local = batch_index - first_row
    is_owned = (batch_local >= 0) & (batch_local < row_count)
    batch_slot = jnp.where(is_owned, batch_local, row_count)
    updated = coefficients.at[:, batch_slot].add(-step_rate * gradient, mode="drop")
    updated = updated.at[:, subset_local].add(step_rate * correction)
    return (predicted, updated)


def solution(mesh):
    rows, cls = mesh.shape["rows"], mesh.shape["cls"]

    def shards(*args):
        cols = args[2].shape[0]
        fits = rows % NX == 0 and cls == 2 * NCORE and cols % 128 == 0
        if fits:
            return fused_shards(rows, cls, *args)
        return plain_shards(*args)

    return jax.shard_map(
        shards,
        mesh=mesh,
        in_specs=(
            P("rows", "cls"), P("cls", "rows"), P("rows", "cls"), P(), P(),
            P("rows"), P("rows", None), P(),
        ),
        out_specs=(P("cls", None), P("cls", "rows")),
        check_vma=False,
    )
```

time: 230 us -> 96.3 us (0.42)
  waiting for transfers between devices: 136 us -> 0 us
  Pallas kernels: 0 us -> 91.5 us
  blocking collectives: 49.7 us -> 0 us
  between operations: 14.2 us -> 0.74 us
  matrix products: 12.2 us -> 0 us
  other arithmetic: 11.5 us -> 0 us
    psum x1 -> x0, waiting for transfers between devices: 129 us -> none  [shards(): predicted, basis_sum = lax.psum((partial_pred, basis_part), 'rows')]
    pallas_call x0 -> x1, Pallas kernels: none -> 91.5 us  [fused_shards(): pl.pallas_call(functools.partial(fused_kernel, rows, cls, class_count), o...]
    all_gather x3 -> x0, blocking collectives: 49.7 us -> none  [the longest x1 31.9 us: shards(): batch_rows = lax.all_gather(batch_features, 'rows', axis=0, tiled=True)]
    dot_general x6 -> x0, matrix products: 12.2 us -> none  [the longest x1 3.83 us: shards(): projected = jnp.dot(gradient, basis_sum.T, precision=lax.Precision.HIGHEST)]
    scatter-add x2 -> x0, other arithmetic: 7.95 us -> none  [the longest x1 6.89 us: shards(): coefficients.at[:, batch_slot].add(-step_rate * gradient, mode='drop')]
    all_gather x1 -> x0, waiting for transfers between devices: 6.52 us -> none  [shards(): batch_whole = lax.all_gather(batch_rows, 'cls', axis=1, tiled=True)]
    reduce_sum x3 -> x0, other arithmetic: 2.82 us -> none  [square_norm(): return jnp.sum(jnp.square(features.astype(jnp.float32)), axis=1)]
    unnamed x21 -> x16, local copies, waits for them, and re-layouts: 4.91 us -> 3.9 us
  transfers between devices with their start and end apart: 2 -> 0, of which waited for: 2 -> 0; matrix products, arithmetic and copies ran while one was open for 1% -> 0% of each run, Pallas kernels for 0% -> 0%
where the time goes in v1:
time: 96.3 us; the launch traced here: 96.1 us
  Pallas kernels  91.5 us (95%)
  local copies, waits for them, and re-layouts  3.9 us (4%)
    pallas_call x1, Pallas kernels, fused_shards(): pl.pallas_call(functools.partial(fused_kernel, rows, cls, class_count), o...  91.5 us
    unnamed x16, local copies, waits for them, and re-layouts  3.9 us

profile of v1, /device:TPU:0, one launch (start us, length us, event | category | flops | bytes accessed | tf_op | source)
XLA Modules:
  0.0 96.1 jit_solution(4448443960538309372)
XLA Ops:
  0.6 0.0 copy-start
  0.6 1.0 %copy.11.bat_ref = bf16[128,320]{1,0:T(8,128)(2,1)S(1)} copy(bf16[128,320]{0,1:T(8,128)(2,1)} %param.10) | data formatting | bytes 163840 | tf_op args[2]
  1.7 0.0 copy-start.1
  1.7 0.0 copy-start.2
  1.7 0.0 copy-start.3
  1.7 0.0 copy-start.4
  1.7 0.0 copy-start.5
  1.7 1.1 %copy.10.cen_ref = bf16[256,320]{1,0:T(8,128)(2,1)S(1)} copy(bf16[256,320]{0,1:T(8,128)(2,1)} %param.8) | data formatting | bytes 327680 | tf_op args[0]
  2.9 0.0 copy-done
  2.9 0.0 copy-done.1
  2.9 0.0 copy-done.2
  2.9 0.0 copy-done.3
  2.9 0.0 copy-done.4
  2.9 0.0 copy-done.5
  3.0 91.5 %shard_map.95 = (f32[250,1024]{1,0:T(8,128)S(1)}, f32[250,256]{1,0:T(8,128)S(1)}) custom-call(bf16[256,320]{1,0:T(8,128)(2,1)S(1)} %copy.10.cen_ref, f32[250,256]{1,0:T(8,128)S(1)} %copy-done, bf16[128,320]{1,0:T(8,128)(2,1)S(1)} %copy.11.bat_ref, s32[8,128]{1,0:T(8,128)S(1)} %bitcast.4, s32[8,128]{1,0:T(8,128)S(1)} %bitcast.5, s32[1,64]{1,0:T(1,128)S(1)} %bitcast.7, ...), custom_call_target="tpu_custom_call" | custom-call | tf_op jit(solution)/shard_map/pallas_call | solution.py:289
  94.5 1.0 %copy.14 = f32[250,1024]{1,0:T(8,128)} copy(f32[250,1024]{1,0:T(8,128)S(1)} %get-tuple-element.4) | data formatting | bytes 2048000
  95.4 0.7 copy.15
Async XLA Ops:
  0.6 2.3 %copy-start = (f32[250,256]{1,0:T(8,128)S(1)}, f32[250,256]{1,0:T(8,128)}, u32[]{:S(2)}) copy-start(f32[250,256]{1,0:T(8,128)} %coef_ref.1) | copy-start | bytes 768004
  1.7 1.2 %copy-start.1 = (f32[64,512]{1,0:T(8,128)S(1)}, f32[64,512]{1,0:T(8,128)}, u32[]{:S(2)}) copy-start(f32[64,512]{1,0:T(8,128)} %eig_ref.1) | copy-start | bytes 393220
  1.7 1.2 %copy-start.2 = (s32[1024]{0:T(1024)S(1)}, s32[1024]{0:T(1024)}, u32[]{:S(2)}) copy-start(s32[1024]{0:T(1024)} %param.11) | copy-start | bytes 12292
  1.7 1.2 %copy-start.3 = (s32[1024]{0:T(1024)S(1)}, s32[1024]{0:T(1024)}, u32[]{:S(2)}) copy-start(s32[1024]{0:T(1024)} %param.12) | copy-start | bytes 12292
  1.7 1.2 %copy-start.4 = (f32[512]{0:T(512)S(1)}, f32[512]{0:T(512)}, u32[]{:S(2)}) copy-start(f32[512]{0:T(512)} %param.15) | copy-start | bytes 6148
  1.7 1.2 %copy-start.5 = (s32[64]{0:T(128)S(1)}, s32[64]{0:T(128)}, u32[]{:S(2)}) copy-start(s32[64]{0:T(128)} %param.13) | copy-start | bytes 772

commit v2 on v0

v2 whole, which is shorter than its diff:
```python
import functools

import jax
import jax.numpy as jnp
from jax import lax
from jax.experimental import pallas as pl
from jax.experimental.pallas import tpu as pltpu
from jax.sharding import PartitionSpec as P

spread = 4.0
step_rate = 0.5
HIGHEST = lax.Precision.HIGHEST
MESH = pl.DeviceIdType.MESH
NX = 2
NCORE = 2
LARGEST = 32767.0
STEPS = 256.0


def kernel_block(inner, row_norm, col_norm):
    squared = row_norm + col_norm - 2.0 * inner
    return jnp.exp(-jnp.sqrt(jnp.maximum(squared, 0.0)) / spread)


def square_norm(features):
    return jnp.sum(jnp.square(features.astype(jnp.float32)), axis=1)


def dot_nt(a, b):
    return lax.dot_general(
        a, b, (((1,), (1,)), ((), ())), preferred_element_type=jnp.float32
    )


def dot_nn(a, b):
    return jnp.dot(a, b, preferred_element_type=jnp.float32)


def split(value):
    high = value.astype(jnp.bfloat16)
    low = (value - high.astype(jnp.float32)).astype(jnp.bfloat16)
    return high, low


def pack(value, slot):
    count = value.shape[0]
    top = jnp.maximum(jnp.max(jnp.abs(value), axis=0, keepdims=True), 1e-37)
    code = jnp.clip(jnp.ceil(jnp.log2(top) * STEPS) + 1.0, -32000.0, 32000.0)
    gain = LARGEST * jnp.exp2(-code / STEPS)
    level = jnp.clip(jnp.round(value * gain), -LARGEST, LARGEST)
    slot[0:count, :] = level.astype(jnp.int32).astype(jnp.int16)
    codes = jnp.broadcast_to(code, (16, value.shape[1]))
    slot[count:count + 16, :] = codes.astype(jnp.int32).astype(jnp.int16)


def unpack(slot):
    count = slot.shape[0] - 16
    codes = slot[count:count + 16, :].astype(jnp.int32).astype(jnp.float32)
    unit = jnp.exp2(codes[0:1, :] / STEPS) / LARGEST
    return slot[0:count, :].astype(jnp.int32).astype(jnp.float32) * unit


def fused_kernel(
    rows, cls, class_count,
    cen_ref, coef_ref, bat_ref, lab_ref, idx_ref, sub_ref, eig_ref, scale_ref,
    pred_ref, new_ref,
    batch, cen, eig, sk, xsend, xrecv, acc, zsend, zrecv, pred, eall, upd,
    send_sem, recv_sem,
):
    nz = rows // NX
    r = lax.axis_index("rows")
    c = lax.axis_index("cls")
    z, x = r // NX, r % NX
    y, k = c // NCORE, c % NCORE
    flip = 1 - 2 * x
    cy = (1 - y) * NCORE + k
    ck = y * NCORE + (1 - k)
    cyk = (1 - y) * NCORE + (1 - k)
    width, row_count = cen_ref.shape
    cols = bat_ref.shape[1]
    subset_count = eig_ref.shape[0]
    eig_part = subset_count // cls
    padded = upd.shape[0]
    first_row = r * row_count
    x_dev, y_dev, k_dev = (r + flip, c), (r, cy), (r, ck)
    near = [lax.rem(z + nz - d, nz) * NX + x for d in range(nz)]
    far = [row + flip for row in near]
    ahead = [lax.rem(z + d, nz) for d in range(nz)]

    def z_dev(d):
        return (ahead[d] * NX + x, c)

    barrier = pltpu.get_barrier_semaphore()
    partners = [x_dev, y_dev, k_dev] + [z_dev(d) for d in range(1, nz)]
    for dev in partners:
        pl.semaphore_signal(barrier, inc=1, device_id=dev, device_id_type=MESH)

    def part(col):
        return pl.ds(pl.multiple_of(col * width, width), width)

    batch[r, part(c), :] = bat_ref[...]
    cen[part(c), :] = cen_ref[...]
    eig_rows = pl.ds(pl.multiple_of(c * eig_part, eig_part), eig_part)
    eig[r, c] = eig_ref[eig_rows, :]
    coef = coef_ref[...]
    if padded > class_count:
        upd[...] = jnp.zeros_like(upd)
        upd[0:class_count, :] = coef
        coef = upd[...]
    coef_high, coef_low = split(coef)
    subset_local = sub_ref[...] - first_row
    pick_t = jnp.transpose(
        (
            lax.broadcasted_iota(jnp.int32, (row_count, subset_count), 0) == subset_local
        ).astype(jnp.float32)
    ).astype(jnp.bfloat16)
    pl.semaphore_wait(barrier, len(partners))

    sent = []

    def send(src, dst, dev):
        n = len(sent)
        copy = pltpu.make_async_remote_copy(
            src_ref=src, dst_ref=dst, send_sem=send_sem.at[n], recv_sem=recv_sem.at[n],
            device_id=dev, device_id_type=MESH,
        )
        copy.start()
        sent.append(copy)

        def arrive(slot):
            pltpu.make_async_remote_copy(
                src_ref=slot, dst_ref=slot, send_sem=send_sem.at[n], recv_sem=recv_sem.at[n],
                device_id=dev, device_id_type=MESH,
            ).wait_recv()

        return arrive

    def slot(row, col):
        return batch.at[row, part(col)]

    def pass_on(row, col, dev):
        return send(slot(row, col), slot(row, col), dev)

    z_in = [None] + [pass_on(r, c, z_dev(d)) for d in range(1, nz)]
    y_in = [pass_on(r, c, y_dev)]
    x_in = [pass_on(r, c, x_dev)]
    cen_y = send(cen.at[part(c)], cen.at[part(c)], y_dev)
    cen_k = send(cen.at[part(c)], cen.at[part(c)], k_dev)
    near_in = [[pass_on(r, c, k_dev)]]
    for d in range(1, nz):
        z_in[d](slot(near[d], c))
        y_in.append(pass_on(near[d], c, y_dev))
        x_in.append(pass_on(near[d], c, x_dev))
        near_in.append([pass_on(near[d], c, k_dev)])
    cen_y(cen.at[part(cy)])
    cen_yk = send(cen.at[part(cy)], cen.at[part(cy)], k_dev)
    xy_in = []
    for d in range(nz):
        y_in[d](slot(near[d], cy))
        xy_in.append(pass_on(near[d], cy, x_dev))
        near_in[d].append(pass_on(near[d], cy, k_dev))
    own_eig = eig.at[r, c]
    ez_in = [None] + [send(own_eig, own_eig, z_dev(d)) for d in range(1, nz)]
    far_in = [[] for _ in range(nz)]

    cen_k(cen.at[part(ck)])
    cen_yk(cen.at[part(cyk)])
    cen_wide = jnp.transpose(cen[...].astype(jnp.float32))
    cen_norm = jnp.sum(cen_wide * cen_wide, axis=1, keepdims=True)
    cen_rows = cen_wide.astype(jnp.bfloat16)

    def part_pred(first, second):
        both = jnp.concatenate([batch[first], batch[second]], axis=1)
        wide = both.astype(jnp.float32)
        norm = jnp.sum(wide * wide, axis=0, keepdims=True)
        high, low = split(kernel_block(dot_nn(cen_rows, both), cen_norm, norm))
        sk_high = dot_nn(pick_t, high).astype(jnp.bfloat16)
        sk_low = dot_nn(pick_t, low).astype(jnp.bfloat16)
        for at, row in enumerate((first, second)):
            lanes = slice(at * cols, (at + 1) * cols)
            sk[row, 0:subset_count, :] = sk_high[:, lanes]
            sk[row, subset_count:2 * subset_count, :] = sk_low[:, lanes]
        return dot_nn(coef_high, high) + dot_nn(coef_high, low) + dot_nn(coef_low, high)

    sum_in = []
    for d in range(0, nz, 2):
        for i in (d, d + 1):
            x_in[i](slot(far[i], c))
            far_in[i].append(pass_on(far[i], c, k_dev))
        for i in (d, d + 1):
            near_in[i][0](slot(near[i], ck))
            near_in[i][1](slot(near[i], cyk))
        both = part_pred(near[d], near[d + 1])
        for at, i in enumerate((d, d + 1)):
            pack(both[:, at * cols:(at + 1) * cols], xsend.at[i])
    for i in range(nz):
        xy_in[i](slot(far[i], cy))
        far_in[i].append(pass_on(far[i], cy, k_dev))
    for i in range(nz):
        sum_in.append(send(xsend.at[i], xrecv.at[i], x_dev))
    ex_in = [send(own_eig, own_eig, x_dev)]
    for d in range(1, nz):
        ez_in[d](eig.at[near[d], c])
        ex_in.append(send(eig.at[near[d], c], eig.at[near[d], c], x_dev))
    for d in range(0, nz, 2):
        for i in (d, d + 1):
            far_in[i][0](slot(far[i], ck))
            far_in[i][1](slot(far[i], cyk))
        both = part_pred(far[d], far[d + 1])
        for at, i in enumerate((d, d + 1)):
            acc[i] = both[:, at * cols:(at + 1) * cols]

    rs_in = [None] * nz
    for d in range(1, nz):
        sum_in[d](xrecv.at[d])
        pack(acc[d] + unpack(xrecv.at[d]), zsend.at[d - 1])
        rs_in[d] = send(zsend.at[d - 1], zrecv.at[d - 1], z_dev(nz - d))
    sum_in[0](xrecv.at[0])
    total = acc[0] + unpack(xrecv.at[0])

    ey_in, ek_in = [], []

    def eig_on(row):
        ey_in.append((send(eig.at[row, c], eig.at[row, c], y_dev), row))
        ek_in.append((send(eig.at[row, c], eig.at[row, c], k_dev), row, ck))

    for row in near:
        eig_on(row)
    for arrive, row in zip(ex_in, far):
        arrive(eig.at[row, c])
        eig_on(row)

    for d in range(1, nz):
        rs_in[d](zrecv.at[d - 1])
        total += unpack(zrecv.at[d - 1])
    mine = far[0]
    pack(total, pred.at[mine])

    pz_in = [None] + [send(pred.at[mine], pred.at[mine], z_dev(d)) for d in range(1, nz)]
    px_in = [send(pred.at[mine], pred.at[mine], x_dev)]

    for arrive, row in ey_in:
        arrive(eig.at[row, cy])
        ek_in.append((send(eig.at[row, cy], eig.at[row, cy], k_dev), row, cyk))

    class_ids = lax.broadcasted_iota(jnp.int32, (padded, cols), 0) + c * class_count
    center_ids = lax.broadcasted_iota(jnp.int32, (row_count, cols), 0) + first_row

    def use_pair(pair, error, update):
        grads, hits, kernels = [], [], []
        for row in pair:
            value = unpack(pred.at[row])
            pred_ref[:, pl.ds(pl.multiple_of(row * cols, cols), cols)] = value[0:class_count]
            grads.append(value - (lab_ref[pl.ds(row, 1), :] == class_ids).astype(jnp.float32))
            hits.append((idx_ref[pl.ds(row, 1), :] == center_ids).astype(jnp.float32))
            kernels.append(sk[row])
        high, low = split(jnp.concatenate(grads, axis=1))
        hit = jnp.concatenate(hits, axis=1).astype(jnp.bfloat16)
        kernel_pair = jnp.concatenate(kernels, axis=1)
        two = dot_nt(kernel_pair, high)
        error += two[0:subset_count] + two[subset_count:]
        error += dot_nt(kernel_pair[0:subset_count], low)
        return error, update + dot_nt(high, hit) + dot_nt(low, hit)

    error = jnp.zeros((subset_count, padded), jnp.float32)
    update = jnp.zeros((padded, row_count), jnp.float32)
    for d in range(0, nz, 2):
        for i in (d, d + 1):
            if i > 0:
                pz_in[i](pred.at[far[i]])
                px_in.append(send(pred.at[far[i]], pred.at[far[i]], x_dev))
        error, update = use_pair((far[d], far[d + 1]), error, update)
    for arrive, row, col in ek_in:
        arrive(eig.at[row, col])
    whole_high, whole_low = split(eig[...].reshape(rows * subset_count, eig_ref.shape[1]))
    own_high, own_low = split(eig_ref[...] * scale_ref[...])
    metric = dot_nt(own_high, whole_high) + dot_nt(own_high, whole_low)
    metric_high, metric_low = split(metric + dot_nt(own_low, whole_high))
    for d in range(0, nz, 2):
        for i in (d, d + 1):
            px_in[i](pred.at[near[i]])
        error, update = use_pair((near[d], near[d + 1]), error, update)

    eall[r] = error
    fz_in = [None] + [send(eall.at[r], eall.at[r], z_dev(d)) for d in range(1, nz)]
    fx_in = [send(eall.at[r], eall.at[r], x_dev)]
    upd[...] = coef - step_rate * update
    for d in range(1, nz):
        fz_in[d](eall.at[near[d]])
        fx_in.append(send(eall.at[near[d]], eall.at[near[d]], x_dev))
    for d in range(nz):
        fx_in[d](eall.at[far[d]])
    high, low = split(eall[...].reshape(rows * subset_count, padded))
    correction = dot_nn(metric_high, high) + dot_nn(metric_high, low) + dot_nn(metric_low, high)
    high, low = split(jnp.transpose(correction))
    moved = dot_nn(high, pick_t) + dot_nn(low, pick_t)
    new_ref[...] = (upd[...] + step_rate * moved)[0:class_count]
    for copy in sent:
        copy.wait_send()


def fused_shards(
    rows, cls,
    centers, coefficients, batch_features, batch_labels, batch_index,
    subset_index, eigen_vectors, eigen_scale,
):
    row_count, width = centers.shape
    class_count = coefficients.shape[0]
    cols = batch_features.shape[0]
    subset_count, eig_count = eigen_vectors.shape
    padded = -(-class_count // 16) * 16
    nz = rows // NX
    copies = 13 * rows + 40
    f32, short = jnp.float32, jnp.int16
    vmem = pl.BlockSpec(memory_space=pltpu.VMEM)
    return pl.pallas_call(
        functools.partial(fused_kernel, rows, cls, class_count),
        out_shape=(
            jax.ShapeDtypeStruct((class_count, rows * cols), f32),
            jax.ShapeDtypeStruct((class_count, row_count), f32),
        ),
        in_specs=[vmem] * 8,
        out_specs=(vmem, vmem),
        scratch_shapes=[
            pltpu.VMEM((rows, cls * width, cols), jnp.bfloat16),
            pltpu.VMEM((cls * width, row_count), jnp.bfloat16),
            pltpu.VMEM((rows, cls, subset_count // cls, eig_count), f32),
            pltpu.VMEM((rows, 2 * subset_count, cols), jnp.bfloat16),
            pltpu.VMEM((nz, padded + 16, cols), short),
            pltpu.VMEM((nz, padded + 16, cols), short),
            pltpu.VMEM((nz, padded, cols), f32),
            pltpu.VMEM((nz - 1, padded + 16, cols), short),
            pltpu.VMEM((nz - 1, padded + 16, cols), short),
            pltpu.VMEM((rows, padded + 16, cols), short),
            pltpu.VMEM((rows, subset_count, padded), f32),
            pltpu.VMEM((padded, row_count), f32),
            pltpu.SemaphoreType.DMA((copies,)),
            pltpu.SemaphoreType.DMA((copies,)),
        ],
        compiler_params=pltpu.CompilerParams(
            collective_id=0, has_side_effects=True, vmem_limit_bytes=48 * 1024 * 1024
        ),
    )(
        centers.T, coefficients, batch_features.T,
        batch_labels.reshape(rows, cols), batch_index.reshape(rows, cols),
        subset_index.reshape(1, subset_count), eigen_vectors,
        eigen_scale.reshape(1, eig_count),
    )


def plain_shards(
    centers, coefficients, batch_features, batch_labels, batch_index,
    subset_index, eigen_vectors, eigen_scale,
):
    row_count = centers.shape[0]
    first_row = lax.axis_index("rows") * row_count
    subset_local = subset_index - first_row
    batch_rows = lax.all_gather(batch_features, "rows", axis=0, tiled=True)
    batch_whole = lax.all_gather(batch_rows, "cls", axis=1, tiled=True)
    batch_norm = square_norm(batch_whole)
    center_whole = lax.all_gather(centers, "cls", axis=1, tiled=True)
    inner = jnp.einsum("cd,bd->cb", center_whole, batch_whole, preferred_element_type=jnp.float32)
    kernel_centers = kernel_block(
        inner, square_norm(center_whole)[:, None], batch_norm[None, :]
    )
    subset_kernel = kernel_centers[subset_local]
    partial_pred = jnp.dot(coefficients, kernel_centers, precision=HIGHEST)
    class_count = coefficients.shape[0]
    class_start = lax.axis_index("cls") * class_count
    class_ids = jnp.arange(class_count, dtype=jnp.int32) + class_start
    targets = (batch_labels[None, :] == class_ids[:, None]).astype(jnp.float32)
    basis_part = jnp.dot(eigen_vectors.T, subset_kernel, precision=HIGHEST)
    predicted, basis_sum = lax.psum((partial_pred, basis_part), "rows")
    gradient = predicted - targets
    projected = jnp.dot(gradient, basis_sum.T, precision=HIGHEST)
    correction = jnp.dot(
        projected * eigen_scale[None, :], eigen_vectors.T, precision=HIGHEST
    )
    batch_local = batch_index - first_row
    is_owned = (batch_local >= 0) & (batch_local < row_count)
    batch_slot = jnp.where(is_owned, batch_local, row_count)
    updated = coefficients.at[:, batch_slot].add(-step_rate * gradient, mode="drop")
    updated = updated.at[:, subset_local].add(step_rate * correction)
    return (predicted, updated)


def solution(mesh):
    rows, cls = mesh.shape["rows"], mesh.shape["cls"]

    def shards(*args):
        cols = args[2].shape[0]
        fits = rows % (2 * NX) == 0 and cls == 2 * NCORE and cols % 128 == 0
        if fits:
            return fused_shards(rows, cls, *args)
        return plain_shards(*args)

    return jax.shard_map(
        shards,
        mesh=mesh,
        in_specs=(
            P("rows", "cls"), P("cls", "rows"), P("rows", "cls"), P(), P(),
            P("rows"), P("rows", None), P(),
        ),
        out_specs=(P("cls", None), P("cls", "rows")),
        check_vma=False,
    )
```

time: 230 us -> 66.2 us (0.29)
  waiting for transfers between devices: 136 us -> 0 us
  Pallas kernels: 0 us -> 59.2 us
  blocking collectives: 49.7 us -> 0 us
  between operations: 14.2 us -> 0.68 us
  matrix products: 12.2 us -> 0 us
  other arithmetic: 11.5 us -> 0 us
    psum x1 -> x0, waiting for transfers between devices: 129 us -> none  [shards(): predicted, basis_sum = lax.psum((partial_pred, basis_part), 'rows')]
    pallas_call x0 -> x1, Pallas kernels: none -> 59.2 us  [fused_shards(): pl.pallas_call(functools.partial(fused_kernel, rows, cls, class_count), o...]
    all_gather x3 -> x0, blocking collectives: 49.7 us -> none  [the longest x1 31.9 us: shards(): batch_rows = lax.all_gather(batch_features, 'rows', axis=0, tiled=True)]
    dot_general x6 -> x0, matrix products: 12.2 us -> none  [the longest x1 3.83 us: shards(): projected = jnp.dot(gradient, basis_sum.T, precision=lax.Precision.HIGHEST)]
    scatter-add x2 -> x0, other arithmetic: 7.95 us -> none  [the longest x1 6.89 us: shards(): coefficients.at[:, batch_slot].add(-step_rate * gradient, mode='drop')]
    all_gather x1 -> x0, waiting for transfers between devices: 6.52 us -> none  [shards(): batch_whole = lax.all_gather(batch_rows, 'cls', axis=1, tiled=True)]
    reduce_sum x3 -> x0, other arithmetic: 2.82 us -> none  [square_norm(): return jnp.sum(jnp.square(features.astype(jnp.float32)), axis=1)]
    unnamed x21 -> x18, local copies, waits for them, and re-layouts: 4.91 us -> 6.02 us
  transfers between devices with their start and end apart: 2 -> 0, of which waited for: 2 -> 0; matrix products, arithmetic and copies ran while one was open for 1% -> 0% of each run, Pallas kernels for 0% -> 0%
where the time goes in v2:
time: 66.2 us; the launch traced here: 65.9 us
  Pallas kernels  59.2 us (89%)
  local copies, waits for them, and re-layouts  6.02 us (9%)
  between operations  0.68 us (1%)
    pallas_call x1, Pallas kernels, fused_shards(): pl.pallas_call(functools.partial(fused_kernel, rows, cls, class_count), o...  59.2 us
    unnamed x18, local copies, waits for them, and re-layouts  6.02 us

profile of v2, /device:TPU:0, one launch (start us, length us, event | category | flops | bytes accessed | tf_op | source)
XLA Modules:
  0.0 65.9 jit_solution(2906621348140239396)
XLA Ops:
  0.6 0.0 copy-start.6
  0.6 0.0 copy-start.5
  0.7 0.0 copy-start.4
  0.7 0.0 copy-start.7
  0.7 0.6 copy-done.6
  1.3 0.0 copy-done.5
  1.3 0.0 copy-done.4
  1.4 0.0 copy-done.7
  1.4 0.0 copy-start
  1.4 0.9 %copy-done = f32[250,256]{1,0:T(8,128)S(1)} copy-done((f32[250,256]{1,0:T(8,128)S(1)}, f32[250,256]{1,0:T(8,128)}, u32[]{:S(2)}) %copy-start) | copy-done | bytes 256024
  2.3 0.0 copy-start.1
  2.3 0.9 %copy-done.1 = bf16[256,320]{0,1:T(8,128)(2,1)S(1)} copy-done((bf16[256,320]{0,1:T(8,128)(2,1)S(1)}, bf16[256,320]{0,1:T(8,128)(2,1)}, u32[]{:S(2)}) %copy-start.1) | copy-done | bytes 163864
  3.2 0.0 copy-start.2
  3.2 0.9 %copy-done.2 = f32[64,512]{1,0:T(8,128)S(1)} copy-done((f32[64,512]{1,0:T(8,128)S(1)}, f32[64,512]{1,0:T(8,128)}, u32[]{:S(2)}) %copy-start.2) | copy-done | bytes 131096
  4.1 0.0 copy-start.3
  4.1 0.9 %copy-done.3 = bf16[128,320]{0,1:T(8,128)(2,1)S(1)} copy-done((bf16[128,320]{0,1:T(8,128)(2,1)S(1)}, bf16[128,320]{0,1:T(8,128)(2,1)}, u32[]{:S(2)}) %copy-start.3) | copy-done | bytes 81944
  5.0 59.2 %shard_map.95 = (f32[250,1024]{1,0:T(8,128)S(1)}, f32[250,256]{1,0:T(8,128)S(1)}) custom-call(bf16[320,256]{1,0:T(8,128)(2,1)S(1)} %bitcast.6, f32[250,256]{1,0:T(8,128)S(1)} %copy-done, bf16[320,128]{1,0:T(8,128)(2,1)S(1)} %bitcast.7, s32[8,128]{1,0:T(8,128)S(1)} %bitcast.8, s32[8,128]{1,0:T(8,128)S(1)} %bitcast.9, s32[1,64]{1,0:T(1,128)S(1)} %bitcast.11, ...), custom_call_target="tpu_custom_call" | custom-call | tf_op jit(solution)/shard_map/pallas_call | solution.py:316
  64.3 1.0 %copy.12 = f32[250,1024]{1,0:T(8,128)} copy(f32[250,1024]{1,0:T(8,128)S(1)} %get-tuple-element.4) | data formatting | bytes 2048000
  65.2 0.7 %copy.13 = f32[250,256]{1,0:T(8,128)} copy(f32[250,256]{1,0:T(8,128)S(1)} %get-tuple-element.5) | data formatting | bytes 512000
Async XLA Ops:
  0.6 0.7 %copy-start.6 = (f32[512]{0:T(512)S(1)}, f32[512]{0:T(512)}, u32[]{:S(2)}) copy-start(f32[512]{0:T(512)} %param.15) | copy-start | bytes 6148
  0.6 0.7 %copy-start.5 = (s32[1024]{0:T(1024)S(1)}, s32[1024]{0:T(1024)}, u32[]{:S(2)}) copy-start(s32[1024]{0:T(1024)} %param.12) | copy-start | bytes 12292
  0.7 0.7 %copy-start.4 = (s32[1024]{0:T(1024)S(1)}, s32[1024]{0:T(1024)}, u32[]{:S(2)}) copy-start(s32[1024]{0:T(1024)} %param.11) | copy-start | bytes 12292
  0.7 0.7 %copy-start.7 = (s32[64]{0:T(128)S(1)}, s32[64]{0:T(128)}, u32[]{:S(2)}) copy-start(s32[64]{0:T(128)} %param.13) | copy-start | bytes 772
  1.4 1.0 %copy-start = (f32[250,256]{1,0:T(8,128)S(1)}, f32[250,256]{1,0:T(8,128)}, u32[]{:S(2)}) copy-start(f32[250,256]{1,0:T(8,128)} %coef_ref.1) | copy-start | bytes 768004
  2.3 0.9 %copy-start.1 = (bf16[256,320]{0,1:T(8,128)(2,1)S(1)}, bf16[256,320]{0,1:T(8,128)(2,1)}, u32[]{:S(2)}) copy-start(bf16[256,320]{0,1:T(8,128)(2,1)} %param.8) | copy-start | bytes 491524
  3.2 0.9 %copy-start.2 = (f32[64,512]{1,0:T(8,128)S(1)}, f32[64,512]{1,0:T(8,128)}, u32[]{:S(2)}) copy-start(f32[64,512]{1,0:T(8,128)} %eig_ref.1) | copy-start | bytes 393220
  4.1 0.9 %copy-start.3 = (bf16[128,320]{0,1:T(8,128)(2,1)S(1)}, bf16[128,320]{0,1:T(8,128)(2,1)}, u32[]{:S(2)}) copy-start(bf16[128,320]{0,1:T(8,128)(2,1)} %param.10) | copy-start | bytes 245764

commit v3 on v2

--- a/solution.py
+++ b/solution.py
@@ -62,10 +62,11 @@
 
 def fused_kernel(
     rows, cls, class_count,
-    cen_ref, coef_ref, bat_ref, lab_ref, idx_ref, sub_ref, eig_ref, scale_ref,
+    cen_hbm, coef_hbm, bat_hbm, lab_hbm, idx_hbm, sub_hbm, eig_hbm, scale_hbm,
     pred_ref, new_ref,
     batch, cen, eig, sk, xsend, xrecv, acc, zsend, zrecv, pred, eall, upd,
-    send_sem, recv_sem,
+    coef_ref, lab_ref, idx_ref, sub_ref, eig_ref, scale_ref,
+    send_sem, recv_sem, local_sem,
 ):
     nz = rows // NX
     r = lax.axis_index("rows")
@@ -76,8 +77,8 @@
     cy = (1 - y) * NCORE + k
     ck = y * NCORE + (1 - k)
     cyk = (1 - y) * NCORE + (1 - k)
-    width, row_count = cen_ref.shape
-    cols = bat_ref.shape[1]
+    width, row_count = cen_hbm.shape
+    cols = bat_hbm.shape[1]
     subset_count = eig_ref.shape[0]
     eig_part = subset_count // cls
     padded = upd.shape[0]
@@ -98,10 +99,54 @@
     def part(col):
         return pl.ds(pl.multiple_of(col * width, width), width)
 
-    batch[r, part(c), :] = bat_ref[...]
-    cen[part(c), :] = cen_ref[...]
     eig_rows = pl.ds(pl.multiple_of(c * eig_part, eig_part), eig_part)
-    eig[r, c] = eig_ref[eig_rows, :]
+    own_eig = eig_hbm.at[eig_rows]
+    local = [
+        pltpu.make_async_copy(src, dst, local_sem.at[n])
+        for n, (src, dst) in enumerate((
+            (sub_hbm, sub_ref), (cen_hbm, cen.at[part(c)]), (bat_hbm, batch.at[r, part(c)]),
+            (coef_hbm, coef_ref), (lab_hbm, lab_ref), (idx_hbm, idx_ref),
+            (eig_hbm, eig_ref), (own_eig, eig.at[r, c]), (scale_hbm, scale_ref),
+        ))
+    ]
+    for copy in local:
+        copy.start()
+    pl.semaphore_wait(barrier, len(partners))
+
+    sent = []
+
+    def send(src, dst, dev):
+        n = len(sent)
+        copy = pltpu.make_async_remote_copy(
+            src_ref=src, dst_ref=dst, send_sem=send_sem.at[n], recv_sem=recv_sem.at[n],
+            device_id=dev, device_id_type=MESH,
+        )
+        copy.start()
+        sent.append(copy)
+
+        def arrive(slot):
+            pltpu.make_async_remote_copy(
+                src_ref=slot, dst_ref=slot, send_sem=send_sem.at[n], recv_sem=recv_sem.at[n],
+                device_id=dev, device_id_type=MESH,
+            ).wait_recv()
+
+        return arrive
+
+    def slot(row, col):
+        return batch.at[row, part(col)]
+
+    def pass_on(row, col, dev):
+        return send(slot(row, col), slot(row, col), dev)
+
+    z_in = [None] + [send(bat_hbm, slot(r, c), z_dev(d)) for d in range(1, nz)]
+    x_in = [send(bat_hbm, slot(r, c), x_dev)]
+    y_in = [send(bat_hbm, slot(r, c), y_dev)]
+    cen_y = send(cen_hbm, cen.at[part(c)], y_dev)
+    near_in = [[send(bat_hbm, slot(r, c), k_dev)]]
+    cen_k = send(cen_hbm, cen.at[part(c)], k_dev)
+
+    for copy in local:
+        copy.wait()
     coef = coef_ref[...]
     if padded > class_count:
         upd[...] = jnp.zeros_like(upd)
@@ -114,39 +159,6 @@
             lax.broadcasted_iota(jnp.int32, (row_count, subset_count), 0) == subset_local
         ).astype(jnp.float32)
     ).astype(jnp.bfloat16)
-    pl.semaphore_wait(barrier, len(partners))
-
-    sent = []
-
-    def send(src, dst, dev):
-        n = len(sent)
-        copy = pltpu.make_async_remote_copy(
-            src_ref=src, dst_ref=dst, send_sem=send_sem.at[n], recv_sem=recv_sem.at[n],
-            device_id=dev, device_id_type=MESH,
-        )
-        copy.start()
-        sent.append(copy)
-
-        def arrive(slot):
-            pltpu.make_async_remote_copy(
-                src_ref=slot, dst_ref=slot, send_sem=send_sem.at[n], recv_sem=recv_sem.at[n],
-                device_id=dev, device_id_type=MESH,
-            ).wait_recv()
-
-        return arrive
-
-    def slot(row, col):
-        return batch.at[row, part(col)]
-
-    def pass_on(row, col, dev):
-        return send(slot(row, col), slot(row, col), dev)
-
-    z_in = [None] + [pass_on(r, c, z_dev(d)) for d in range(1, nz)]
-    y_in = [pass_on(r, c, y_dev)]
-    x_in = [pass_on(r, c, x_dev)]
-    cen_y = send(cen.at[part(c)], cen.at[part(c)], y_dev)
-    cen_k = send(cen.at[part(c)], cen.at[part(c)], k_dev)
-    near_in = [[pass_on(r, c, k_dev)]]
     for d in range(1, nz):
         z_in[d](slot(near[d], c))
         y_in.append(pass_on(near[d], c, y_dev))
@@ -157,10 +169,10 @@
     xy_in = []
     for d in range(nz):
         y_in[d](slot(near[d], cy))
-        xy_in.append(pass_on(near[d], cy, x_dev))
+        if d < nz - 1:
+            xy_in.append(pass_on(near[d], cy, x_dev))
         near_in[d].append(pass_on(near[d], cy, k_dev))
-    own_eig = eig.at[r, c]
-    ez_in = [None] + [send(own_eig, own_eig, z_dev(d)) for d in range(1, nz)]
+    ez_in = [None] + [send(own_eig, eig.at[r, c], z_dev(d)) for d in range(1, nz)]
     far_in = [[] for _ in range(nz)]
 
     cen_k(cen.at[part(ck)])
@@ -182,23 +194,24 @@
             sk[row, subset_count:2 * subset_count, :] = sk_low[:, lanes]
         return dot_nn(coef_high, high) + dot_nn(coef_high, low) + dot_nn(coef_low, high)
 
+    for i in range(nz - 1, -1, -1):
+        x_in[i](slot(far[i], c))
+        if i == nz - 1:
+            xy_in.append(pass_on(far[i], c, y_dev))
+        far_in[i].append(pass_on(far[i], c, k_dev))
     sum_in = []
     for d in range(0, nz, 2):
-        for i in (d, d + 1):
-            x_in[i](slot(far[i], c))
-            far_in[i].append(pass_on(far[i], c, k_dev))
         for i in (d, d + 1):
             near_in[i][0](slot(near[i], ck))
             near_in[i][1](slot(near[i], cyk))
         both = part_pred(near[d], near[d + 1])
         for at, i in enumerate((d, d + 1)):
             pack(both[:, at * cols:(at + 1) * cols], xsend.at[i])
-    for i in range(nz):
-        xy_in[i](slot(far[i], cy))
-        far_in[i].append(pass_on(far[i], cy, k_dev))
-    for i in range(nz):
-        sum_in.append(send(xsend.at[i], xrecv.at[i], x_dev))
-    ex_in = [send(own_eig, own_eig, x_dev)]
+            sum_in.append(send(xsend.at[i], xrecv.at[i], x_dev))
+        for i in (d, d + 1):
+            xy_in[i](slot(far[i], cy))
+            far_in[i].append(pass_on(far[i], cy, k_dev))
+    ex_in = [send(own_eig, eig.at[r, c], x_dev)]
     for d in range(1, nz):
         ez_in[d](eig.at[near[d], c])
         ex_in.append(send(eig.at[near[d], c], eig.at[near[d], c], x_dev))
@@ -281,7 +294,7 @@
             px_in[i](pred.at[near[i]])
         error, update = use_pair((near[d], near[d + 1]), error, update)
 
-    eall[r] = error
+    pack(error, eall.at[r])
     fz_in = [None] + [send(eall.at[r], eall.at[r], z_dev(d)) for d in range(1, nz)]
     fx_in = [send(eall.at[r], eall.at[r], x_dev)]
     upd[...] = coef - step_rate * update
@@ -290,7 +303,7 @@
         fx_in.append(send(eall.at[near[d]], eall.at[near[d]], x_dev))
     for d in range(nz):
         fx_in[d](eall.at[far[d]])
-    high, low = split(eall[...].reshape(rows * subset_count, padded))
+    high, low = split(jnp.concatenate([unpack(eall.at[row]) for row in range(rows)], axis=0))
     correction = dot_nn(metric_high, high) + dot_nn(metric_high, low) + dot_nn(metric_low, high)
     high, low = split(jnp.transpose(correction))
     moved = dot_nn(high, pick_t) + dot_nn(low, pick_t)
@@ -319,7 +332,7 @@
             jax.ShapeDtypeStruct((class_count, rows * cols), f32),
             jax.ShapeDtypeStruct((class_count, row_count), f32),
         ),
-        in_specs=[vmem] * 8,
+        in_specs=[pl.BlockSpec(memory_space=pltpu.HBM)] * 8,
         out_specs=(vmem, vmem),
         scratch_shapes=[
             pltpu.VMEM((rows, cls * width, cols), jnp.bfloat16),
@@ -332,10 +345,17 @@
             pltpu.VMEM((nz - 1, padded + 16, cols), short),
             pltpu.VMEM((nz - 1, padded + 16, cols), short),
             pltpu.VMEM((rows, padded + 16, cols), short),
-            pltpu.VMEM((rows, subset_count, padded), f32),
+            pltpu.VMEM((rows, subset_count + 16, padded), short),
             pltpu.VMEM((padded, row_count), f32),
+            pltpu.VMEM((class_count, row_count), f32),
+            pltpu.VMEM((rows, cols), jnp.int32),
+            pltpu.VMEM((rows, cols), jnp.int32),
+            pltpu.VMEM((1, subset_count), jnp.int32),
+            pltpu.VMEM((subset_count, eig_count), f32),
+            pltpu.VMEM((1, eig_count), f32),
             pltpu.SemaphoreType.DMA((copies,)),
             pltpu.SemaphoreType.DMA((copies,)),
+            pltpu.SemaphoreType.DMA((9,)),
         ],
         compiler_params=pltpu.CompilerParams(
             collective_id=0, has_side_effects=True, vmem_limit_bytes=48 * 1024 * 1024

time: 66.2 us -> 62.7 us (0.947)
  Pallas kernels: 59.2 us -> 55.2 us
    pallas_call x1, Pallas kernels: 59.2 us -> 55.2 us  [fused_shards(): pl.pallas_call(functools.partial(fused_kernel, rows, cls, class_count), o...]
where the time goes in v3:
time: 62.7 us; the launch traced here: 61.9 us
  Pallas kernels  55.2 us (88%)
  local copies, waits for them, and re-layouts  6.02 us (10%)
  between operations  0.68 us (1%)
    pallas_call x1, Pallas kernels, fused_shards(): pl.pallas_call(functools.partial(fused_kernel, rows, cls, class_count), o...  55.2 us
    unnamed x18, local copies, waits for them, and re-layouts  6.02 us

profile of v3, /device:TPU:0, one launch (start us, length us, event | category | flops | bytes accessed | tf_op | source)
XLA Modules:
  0.0 61.9 jit_solution(17547815661602810445)
XLA Ops:
  0.6 0.0 copy-start.6
  0.6 0.0 copy-start.5
  0.7 0.0 copy-start.4
  0.7 0.0 copy-start.7
  0.7 0.6 %copy-done.6 = f32[512]{0:T(512)S(1)} copy-done((f32[512]{0:T(512)S(1)}, f32[512]{0:T(512)}, u32[]{:S(2)}) %copy-start.6) | copy-done | bytes 2072
  1.3 0.0 copy-done.5
  1.3 0.0 copy-done.4
  1.4 0.0 copy-done.7
  1.4 0.0 copy-start
  1.4 0.9 %copy-done = f32[250,256]{1,0:T(8,128)S(1)} copy-done((f32[250,256]{1,0:T(8,128)S(1)}, f32[250,256]{1,0:T(8,128)}, u32[]{:S(2)}) %copy-start) | copy-done | bytes 256024
  2.3 0.0 copy-start.1
  2.3 0.9 %copy-done.1 = bf16[256,320]{0,1:T(8,128)(2,1)S(1)} copy-done((bf16[256,320]{0,1:T(8,128)(2,1)S(1)}, bf16[256,320]{0,1:T(8,128)(2,1)}, u32[]{:S(2)}) %copy-start.1) | copy-done | bytes 163864
  3.2 0.0 copy-start.2
  3.2 0.9 %copy-done.2 = f32[64,512]{1,0:T(8,128)S(1)} copy-done((f32[64,512]{1,0:T(8,128)S(1)}, f32[64,512]{1,0:T(8,128)}, u32[]{:S(2)}) %copy-start.2) | copy-done | bytes 131096
  4.1 0.0 copy-start.3
  4.1 0.9 %copy-done.3 = bf16[128,320]{0,1:T(8,128)(2,1)S(1)} copy-done((bf16[128,320]{0,1:T(8,128)(2,1)S(1)}, bf16[128,320]{0,1:T(8,128)(2,1)}, u32[]{:S(2)}) %copy-start.3) | copy-done | bytes 81944
  5.0 55.2 %shard_map.95 = (f32[250,1024]{1,0:T(8,128)S(1)}, f32[250,256]{1,0:T(8,128)S(1)}) custom-call(bf16[320,256]{1,0:T(8,128)(2,1)S(1)} %bitcast.6, f32[250,256]{1,0:T(8,128)S(1)} %copy-done, bf16[320,128]{1,0:T(8,128)(2,1)S(1)} %bitcast.7, s32[8,128]{1,0:T(8,128)S(1)} %bitcast.8, s32[8,128]{1,0:T(8,128)S(1)} %bitcast.9, s32[1,64]{1,0:T(1,128)S(1)} %bitcast.11, ...), custom_call_target="tpu_custom_call" | custom-call | tf_op jit(solution)/shard_map/pallas_call | solution.py:329
  60.2 1.0 %copy.12 = f32[250,1024]{1,0:T(8,128)} copy(f32[250,1024]{1,0:T(8,128)S(1)} %get-tuple-element.4) | data formatting | bytes 2048000
  61.2 0.7 %copy.13 = f32[250,256]{1,0:T(8,128)} copy(f32[250,256]{1,0:T(8,128)S(1)} %get-tuple-element.5) | data formatting | bytes 512000
Async XLA Ops:
  0.6 0.7 %copy-start.6 = (f32[512]{0:T(512)S(1)}, f32[512]{0:T(512)}, u32[]{:S(2)}) copy-start(f32[512]{0:T(512)} %param.15) | copy-start | bytes 6148
  0.6 0.7 %copy-start.5 = (s32[1024]{0:T(1024)S(1)}, s32[1024]{0:T(1024)}, u32[]{:S(2)}) copy-start(s32[1024]{0:T(1024)} %param.12) | copy-start | bytes 12292
  0.7 0.7 %copy-start.4 = (s32[1024]{0:T(1024)S(1)}, s32[1024]{0:T(1024)}, u32[]{:S(2)}) copy-start(s32[1024]{0:T(1024)} %param.11) | copy-start | bytes 12292
  0.7 0.7 %copy-start.7 = (s32[64]{0:T(128)S(1)}, s32[64]{0:T(128)}, u32[]{:S(2)}) copy-start(s32[64]{0:T(128)} %param.13) | copy-start | bytes 772
  1.4 1.0 %copy-start = (f32[250,256]{1,0:T(8,128)S(1)}, f32[250,256]{1,0:T(8,128)}, u32[]{:S(2)}) copy-start(f32[250,256]{1,0:T(8,128)} %coef_hbm.1) | copy-start | bytes 768004
  2.3 0.9 %copy-start.1 = (bf16[256,320]{0,1:T(8,128)(2,1)S(1)}, bf16[256,320]{0,1:T(8,128)(2,1)}, u32[]{:S(2)}) copy-start(bf16[256,320]{0,1:T(8,128)(2,1)} %param.8) | copy-start | bytes 491524
  3.2 0.9 %copy-start.2 = (f32[64,512]{1,0:T(8,128)S(1)}, f32[64,512]{1,0:T(8,128)}, u32[]{:S(2)}) copy-start(f32[64,512]{1,0:T(8,128)} %eig_hbm.1) | copy-start | bytes 393220
  4.1 0.9 %copy-start.3 = (bf16[128,320]{0,1:T(8,128)(2,1)S(1)}, bf16[128,320]{0,1:T(8,128)(2,1)}, u32[]{:S(2)}) copy-start(bf16[128,320]{0,1:T(8,128)(2,1)} %param.10) | copy-start | bytes 245764

commit v4 on v3

--- a/solution.py
+++ b/solution.py
@@ -63,9 +63,9 @@
 def fused_kernel(
     rows, cls, class_count,
     cen_hbm, coef_hbm, bat_hbm, lab_hbm, idx_hbm, sub_hbm, eig_hbm, scale_hbm,
-    pred_ref, new_ref,
+    pred_hbm, new_hbm,
     batch, cen, eig, sk, xsend, xrecv, acc, zsend, zrecv, pred, eall, upd,
-    coef_ref, lab_ref, idx_ref, sub_ref, eig_ref, scale_ref,
+    pred_ref, coef_ref, lab_ref, idx_ref, sub_ref, eig_ref, scale_ref,
     send_sem, recv_sem, local_sem,
 ):
     nz = rows // NX
@@ -259,11 +259,19 @@
     class_ids = lax.broadcasted_iota(jnp.int32, (padded, cols), 0) + c * class_count
     center_ids = lax.broadcasted_iota(jnp.int32, (row_count, cols), 0) + first_row
 
+    leaving = []
+
     def use_pair(pair, error, update):
         grads, hits, kernels = [], [], []
         for row in pair:
             value = unpack(pred.at[row])
-            pred_ref[:, pl.ds(pl.multiple_of(row * cols, cols), cols)] = value[0:class_count]
+            pred_ref[row] = value[0:class_count]
+            columns = pl.ds(pl.multiple_of(row * cols, cols), cols)
+            n = 9 + len(leaving)
+            leaving.append(
+                pltpu.make_async_copy(pred_ref.at[row], pred_hbm.at[:, columns], local_sem.at[n])
+            )
+            leaving[-1].start()
             grads.append(value - (lab_ref[pl.ds(row, 1), :] == class_ids).astype(jnp.float32))
             hits.append((idx_ref[pl.ds(row, 1), :] == center_ids).astype(jnp.float32))
             kernels.append(sk[row])
@@ -307,7 +315,11 @@
     correction = dot_nn(metric_high, high) + dot_nn(metric_high, low) + dot_nn(metric_low, high)
     high, low = split(jnp.transpose(correction))
     moved = dot_nn(high, pick_t) + dot_nn(low, pick_t)
-    new_ref[...] = (upd[...] + step_rate * moved)[0:class_count]
+    coef_ref[...] = (upd[...] + step_rate * moved)[0:class_count]
+    leaving.append(pltpu.make_async_copy(coef_ref, new_hbm, local_sem.at[9 + rows]))
+    leaving[-1].start()
+    for copy in leaving:
+        copy.wait()
     for copy in sent:
         copy.wait_send()
 
@@ -325,15 +337,15 @@
     nz = rows // NX
     copies = 13 * rows + 40
     f32, short = jnp.float32, jnp.int16
-    vmem = pl.BlockSpec(memory_space=pltpu.VMEM)
+    hbm = pl.BlockSpec(memory_space=pltpu.HBM)
     return pl.pallas_call(
         functools.partial(fused_kernel, rows, cls, class_count),
         out_shape=(
             jax.ShapeDtypeStruct((class_count, rows * cols), f32),
             jax.ShapeDtypeStruct((class_count, row_count), f32),
         ),
-        in_specs=[pl.BlockSpec(memory_space=pltpu.HBM)] * 8,
-        out_specs=(vmem, vmem),
+        in_specs=[hbm] * 8,
+        out_specs=(hbm, hbm),
         scratch_shapes=[
             pltpu.VMEM((rows, cls * width, cols), jnp.bfloat16),
             pltpu.VMEM((cls * width, row_count), jnp.bfloat16),
@@ -347,6 +359,7 @@
             pltpu.VMEM((rows, padded + 16, cols), short),
             pltpu.VMEM((rows, subset_count + 16, padded), short),
             pltpu.VMEM((padded, row_count), f32),
+            pltpu.VMEM((rows, class_count, cols), f32),
             pltpu.VMEM((class_count, row_count), f32),
             pltpu.VMEM((rows, cols), jnp.int32),
             pltpu.VMEM((rows, cols), jnp.int32),
@@ -355,10 +368,10 @@
             pltpu.VMEM((1, eig_count), f32),
             pltpu.SemaphoreType.DMA((copies,)),
             pltpu.SemaphoreType.DMA((copies,)),
-            pltpu.SemaphoreType.DMA((9,)),
+            pltpu.SemaphoreType.DMA((rows + 10,)),
         ],
         compiler_params=pltpu.CompilerParams(
-            collective_id=0, has_side_effects=True, vmem_limit_bytes=48 * 1024 * 1024
+            collective_id=0, has_side_effects=True, vmem_limit_bytes=62 * 1024 * 1024
         ),
     )(
         centers.T, coefficients, batch_features.T,

time: 62.7 us -> 60.5 us (0.965)
  local copies, waits for them, and re-layouts: 6.02 us -> 3.06 us
  Pallas kernels: 55.2 us -> 56.3 us
    unnamed x18 -> x4, local copies, waits for them, and re-layouts: 6.02 us -> 3.06 us
    pallas_call x1, Pallas kernels: 55.2 us -> 56.3 us  [fused_shards(): pl.pallas_call(functools.partial(fused_kernel, rows, cls, class_count), o...]
where the time goes in v4:
time: 60.5 us; the launch traced here: 60 us
  Pallas kernels  56.3 us (93%)
  local copies, waits for them, and re-layouts  3.06 us (5%)
  between operations  0.65 us (1%)
    pallas_call x1, Pallas kernels, fused_shards(): pl.pallas_call(functools.partial(fused_kernel, rows, cls, class_count), o...  56.3 us
    unnamed x4, local copies, waits for them, and re-layouts  3.06 us

profile of v4, /device:TPU:0, one launch (start us, length us, event | category | flops | bytes accessed | tf_op | source)
XLA Modules:
  0.0 60.0 jit_solution(11335443433428098560)
XLA Ops:
  0.6 56.3 %shard_map.95 = (f32[250,1024]{1,0:T(8,128)}, f32[250,256]{1,0:T(8,128)}) custom-call(bf16[320,256]{1,0:T(8,128)(2,1)} %bitcast.6, f32[250,256]{1,0:T(8,128)} %coef_hbm.1, bf16[320,128]{1,0:T(8,128)(2,1)} %bitcast.7, s32[8,128]{1,0:T(8,128)} %bitcast.8, s32[8,128]{1,0:T(8,128)} %bitcast.9, s32[1,64]{1,0:T(1,128)} %bitcast.11, f32[64,512]{1,0:T(8,128)} %eig_hbm.1, ...), custom_call_target="tpu_custom_call" | custom-call | tf_op jit(solution)/shard_map/pallas_call | solution.py:341
  56.9 0.0 copy-start
  56.9 2.3 %copy.12 = f32[250,1024]{1,0:T(8,128)} copy(f32[250,1024]{1,0:T(8,128)} %get-tuple-element.4) | data formatting | bytes 2048000
  59.3 0.0 copy-done
  59.3 0.7 %copy.13 = f32[250,256]{1,0:T(8,128)} copy(f32[250,256]{1,0:T(8,128)S(1)} %copy-done) | data formatting | bytes 512000
Async XLA Ops:
  56.9 2.4 %copy-start = (f32[250,256]{1,0:T(8,128)S(1)}, f32[250,256]{1,0:T(8,128)}, u32[]{:S(2)}) copy-start(f32[250,256]{1,0:T(8,128)} %get-tuple-element.5) | copy-start | bytes 768004

commit v5 on v4

--- a/solution.py
+++ b/solution.py
@@ -65,7 +65,7 @@
     cen_hbm, coef_hbm, bat_hbm, lab_hbm, idx_hbm, sub_hbm, eig_hbm, scale_hbm,
     pred_hbm, new_hbm,
     batch, cen, eig, sk, xsend, xrecv, acc, zsend, zrecv, pred, eall, upd,
-    pred_ref, coef_ref, lab_ref, idx_ref, sub_ref, eig_ref, scale_ref,
+    coef_ref, lab_ref, idx_ref, sub_ref, eig_ref, scale_ref,
     send_sem, recv_sem, local_sem,
 ):
     nz = rows // NX
@@ -181,18 +181,25 @@
     cen_norm = jnp.sum(cen_wide * cen_wide, axis=1, keepdims=True)
     cen_rows = cen_wide.astype(jnp.bfloat16)
 
+    later = []
+
     def part_pred(first, second):
         both = jnp.concatenate([batch[first], batch[second]], axis=1)
         wide = both.astype(jnp.float32)
         norm = jnp.sum(wide * wide, axis=0, keepdims=True)
         high, low = split(kernel_block(dot_nn(cen_rows, both), cen_norm, norm))
-        sk_high = dot_nn(pick_t, high).astype(jnp.bfloat16)
-        sk_low = dot_nn(pick_t, low).astype(jnp.bfloat16)
-        for at, row in enumerate((first, second)):
-            lanes = slice(at * cols, (at + 1) * cols)
-            sk[row, 0:subset_count, :] = sk_high[:, lanes]
-            sk[row, subset_count:2 * subset_count, :] = sk_low[:, lanes]
+        later.append((first, second, high, low))
         return dot_nn(coef_high, high) + dot_nn(coef_high, low) + dot_nn(coef_low, high)
+
+    def subset_part():
+        for first, second, high, low in later:
+            sk_high = dot_nn(pick_t, high).astype(jnp.bfloat16)
+            sk_low = dot_nn(pick_t, low).astype(jnp.bfloat16)
+            for at, row in enumerate((first, second)):
+                lanes = slice(at * cols, (at + 1) * cols)
+                sk[row, 0:subset_count, :] = sk_high[:, lanes]
+                sk[row, subset_count:2 * subset_count, :] = sk_low[:, lanes]
+        later.clear()
 
     for i in range(nz - 1, -1, -1):
         x_in[i](slot(far[i], c))
@@ -208,6 +215,7 @@
         for at, i in enumerate((d, d + 1)):
             pack(both[:, at * cols:(at + 1) * cols], xsend.at[i])
             sum_in.append(send(xsend.at[i], xrecv.at[i], x_dev))
+        subset_part()
         for i in (d, d + 1):
             xy_in[i](slot(far[i], cy))
             far_in[i].append(pass_on(far[i], cy, k_dev))
@@ -230,6 +238,7 @@
         rs_in[d] = send(zsend.at[d - 1], zrecv.at[d - 1], z_dev(nz - d))
     sum_in[0](xrecv.at[0])
     total = acc[0] + unpack(xrecv.at[0])
+    subset_part()
 
     ey_in, ek_in = [], []
 
@@ -239,10 +248,6 @@
 
     for row in near:
         eig_on(row)
-    for arrive, row in zip(ex_in, far):
-        arrive(eig.at[row, c])
-        eig_on(row)
-
     for d in range(1, nz):
         rs_in[d](zrecv.at[d - 1])
         total += unpack(zrecv.at[d - 1])
@@ -252,36 +257,41 @@
     pz_in = [None] + [send(pred.at[mine], pred.at[mine], z_dev(d)) for d in range(1, nz)]
     px_in = [send(pred.at[mine], pred.at[mine], x_dev)]
 
-    for arrive, row in ey_in:
-        arrive(eig.at[row, cy])
-        ek_in.append((send(eig.at[row, cy], eig.at[row, cy], k_dev), row, cyk))
+    for arrive, row in zip(ex_in, far):
+        arrive(eig.at[row, c])
+        eig_on(row)
 
     class_ids = lax.broadcasted_iota(jnp.int32, (padded, cols), 0) + c * class_count
     center_ids = lax.broadcasted_iota(jnp.int32, (row_count, cols), 0) + first_row
 
     leaving = []
 
-    def use_pair(pair, error, update):
+    def use_pair(pair, error):
         grads, hits, kernels = [], [], []
         for row in pair:
-            value = unpack(pred.at[row])
-            pred_ref[row] = value[0:class_count]
             columns = pl.ds(pl.multiple_of(row * cols, cols), cols)
             n = 9 + len(leaving)
             leaving.append(
-                pltpu.make_async_copy(pred_ref.at[row], pred_hbm.at[:, columns], local_sem.at[n])
+                pltpu.make_async_copy(pred.at[row], pred_hbm.at[:, columns], local_sem.at[n])
             )
             leaving[-1].start()
+            value = unpack(pred.at[row])
             grads.append(value - (lab_ref[pl.ds(row, 1), :] == class_ids).astype(jnp.float32))
-            hits.append((idx_ref[pl.ds(row, 1), :] == center_ids).astype(jnp.float32))
             kernels.append(sk[row])
         high, low = split(jnp.concatenate(grads, axis=1))
-        hit = jnp.concatenate(hits, axis=1).astype(jnp.bfloat16)
         kernel_pair = jnp.concatenate(kernels, axis=1)
         two = dot_nt(kernel_pair, high)
         error += two[0:subset_count] + two[subset_count:]
-        error += dot_nt(kernel_pair[0:subset_count], low)
-        return error, update + dot_nt(high, hit) + dot_nt(low, hit)
+        return error + dot_nt(kernel_pair[0:subset_count], low), (pair, high, low)
+
+    def scatter(update, moves):
+        for pair, high, low in moves:
+            hit = jnp.concatenate(
+                [(idx_ref[pl.ds(row, 1), :] == center_ids).astype(jnp.float32) for row in pair],
+                axis=1,
+            ).astype(jnp.bfloat16)
+            update += dot_nt(high, hit) + dot_nt(low, hit)
+        return update
 
     error = jnp.zeros((subset_count, padded), jnp.float32)
     update = jnp.zeros((padded, row_count), jnp.float32)
@@ -290,25 +300,32 @@
             if i > 0:
                 pz_in[i](pred.at[far[i]])
                 px_in.append(send(pred.at[far[i]], pred.at[far[i]], x_dev))
-        error, update = use_pair((far[d], far[d + 1]), error, update)
+        error, move = use_pair((far[d], far[d + 1]), error)
+        update = scatter(update, [move])
+    moves = []
+    for d in range(0, nz, 2):
+        for i in (d, d + 1):
+            px_in[i](pred.at[near[i]])
+        error, move = use_pair((near[d], near[d + 1]), error)
+        moves.append(move)
+
+    pack(error, eall.at[r])
+    fz_in = [None] + [send(eall.at[r], eall.at[r], z_dev(d)) for d in range(1, nz)]
+    fx_in = [send(eall.at[r], eall.at[r], x_dev)]
+    for arrive, row in ey_in:
+        arrive(eig.at[row, cy])
+        ek_in.append((send(eig.at[row, cy], eig.at[row, cy], k_dev), row, cyk))
+    upd[...] = coef - step_rate * scatter(update, moves[:1])
+    for d in range(1, nz):
+        fz_in[d](eall.at[near[d]])
+        fx_in.append(send(eall.at[near[d]], eall.at[near[d]], x_dev))
+    upd[...] -= step_rate * scatter(jnp.zeros_like(update), moves[1:])
     for arrive, row, col in ek_in:
         arrive(eig.at[row, col])
     whole_high, whole_low = split(eig[...].reshape(rows * subset_count, eig_ref.shape[1]))
     own_high, own_low = split(eig_ref[...] * scale_ref[...])
     metric = dot_nt(own_high, whole_high) + dot_nt(own_high, whole_low)
     metric_high, metric_low = split(metric + dot_nt(own_low, whole_high))
-    for d in range(0, nz, 2):
-        for i in (d, d + 1):
-            px_in[i](pred.at[near[i]])
-        error, update = use_pair((near[d], near[d + 1]), error, update)
-
-    pack(error, eall.at[r])
-    fz_in = [None] + [send(eall.at[r], eall.at[r], z_dev(d)) for d in range(1, nz)]
-    fx_in = [send(eall.at[r], eall.at[r], x_dev)]
-    upd[...] = coef - step_rate * update
-    for d in range(1, nz):
-        fz_in[d](eall.at[near[d]])
-        fx_in.append(send(eall.at[near[d]], eall.at[near[d]], x_dev))
     for d in range(nz):
         fx_in[d](eall.at[far[d]])
     high, low = split(jnp.concatenate([unpack(eall.at[row]) for row in range(rows)], axis=0))
@@ -338,10 +355,10 @@
     copies = 13 * rows + 40
     f32, short = jnp.float32, jnp.int16
     hbm = pl.BlockSpec(memory_space=pltpu.HBM)
-    return pl.pallas_call(
+    levels, updated = pl.pallas_call(
         functools.partial(fused_kernel, rows, cls, class_count),
         out_shape=(
-            jax.ShapeDtypeStruct((class_count, rows * cols), f32),
+            jax.ShapeDtypeStruct((padded + 16, rows * cols), short),
             jax.ShapeDtypeStruct((class_count, row_count), f32),
         ),
         in_specs=[hbm] * 8,
@@ -359,7 +376,6 @@
             pltpu.VMEM((rows, padded + 16, cols), short),
             pltpu.VMEM((rows, subset_count + 16, padded), short),
             pltpu.VMEM((padded, row_count), f32),
-            pltpu.VMEM((rows, class_count, cols), f32),
             pltpu.VMEM((class_count, row_count), f32),
             pltpu.VMEM((rows, cols), jnp.int32),
             pltpu.VMEM((rows, cols), jnp.int32),
@@ -379,6 +395,8 @@
         subset_index.reshape(1, subset_count), eigen_vectors,
         eigen_scale.reshape(1, eig_count),
     )
+    unit = jnp.exp2(levels[padded:padded + 1].astype(f32) / STEPS) / LARGEST
+    return levels[0:class_count].astype(f32) * unit, updated
 
 
 def plain_shards(

time: 60.5 us -> 61.7 us (1.020)
  other arithmetic: 0 us -> 2.98 us
  local copies, waits for them, and re-layouts: 3.06 us -> 0.71 us
  Pallas kernels: 56.3 us -> 57.1 us
    unnamed x4 -> x3, local copies, waits for them, and re-layouts: 3.06 us -> 0.71 us
    mul x0 -> x1, other arithmetic: none -> 2.24 us  [fused_shards(): return (levels[0:class_count].astype(f32) * unit, updated)]
    pallas_call x1, Pallas kernels: 56.3 us -> 57.1 us  [fused_shards(): pl.pallas_call(functools.partial(fused_kernel, rows, cls, class_count), o...]
    div x0 -> x1, other arithmetic: none -> 0.74 us  [fused_shards(): unit = jnp.exp2(levels[padded:padded + 1].astype(f32) / STEPS) / LARGEST]
where the time goes in v5:
time: 61.7 us; the launch traced here: 61.5 us
  Pallas kernels  57.1 us (93%)
  other arithmetic  2.98 us (5%)
  local copies, waits for them, and re-layouts  0.71 us (1%)
  between operations  0.65 us (1%)
    pallas_call x1, Pallas kernels, fused_shards(): pl.pallas_call(functools.partial(fused_kernel, rows, cls, class_count), o...  57.1 us
    mul x1, other arithmetic, fused_shards(): return (levels[0:class_count].astype(f32) * unit, updated)  2.24 us

profile of v5, /device:TPU:0, one launch (start us, length us, event | category | flops | bytes accessed | tf_op | source)
XLA Modules:
  0.0 61.5 jit_solution(18344198788153851781)
XLA Ops:
  0.6 57.1 %shard_map.95 = (s16[272,1024]{1,0:T(8,128)(2,1)}, f32[250,256]{1,0:T(8,128)}) custom-call(bf16[320,256]{1,0:T(8,128)(2,1)} %bitcast.7, f32[250,256]{1,0:T(8,128)} %coef_hbm.1, bf16[320,128]{1,0:T(8,128)(2,1)} %bitcast.8, s32[8,128]{1,0:T(8,128)} %bitcast.10, s32[8,128]{1,0:T(8,128)} %bitcast.11, s32[1,64]{1,0:T(1,128)} %bitcast.13, f32[64,512]{1,0:T(8,128)} %eig_hbm.1, ...), custom_call_target="tpu_custom_call" | custom-call | tf_op jit(solution)/shard_map/pallas_call | solution.py:358
  57.8 0.7 %exponential_multiply_fusion = f32[1,1024]{1,0:T(1,128)S(1)} fusion(s16[272,1024]{1,0:T(8,128)(2,1)} %get-tuple-element.4), kind=kLoop, calls=%fused_computation.1 | loop fusion | flops 3072 | bytes 6144 | tf_op jit(solution)/shard_map/div | solution.py:398
  58.5 0.0 copy-start
  58.5 2.2 %convert_multiply_fusion = f32[250,1024]{1,0:T(8,128)} fusion(f32[1024]{0:T(1024)S(1)} %bitcast.9, s16[272,1024]{1,0:T(8,128)(2,1)} %get-tuple-element.4), kind=kLoop, calls=%fused_computation | loop fusion | flops 512000 | bytes 1540096 | tf_op jit(solution)/shard_map/mul | solution.py:399
  60.8 0.0 copy-done
  60.8 0.7 %copy.11 = f32[250,256]{1,0:T(8,128)} copy(f32[250,256]{1,0:T(8,128)S(1)} %copy-done) | data formatting | bytes 512000
Async XLA Ops:
  58.5 2.3 %copy-start = (f32[250,256]{1,0:T(8,128)S(1)}, f32[250,256]{1,0:T(8,128)}, u32[]{:S(2)}) copy-start(f32[250,256]{1,0:T(8,128)} %get-tuple-element.9) | copy-start | bytes 768004

commit v6 on v5

--- a/solution.py
+++ b/solution.py
@@ -64,8 +64,8 @@
     rows, cls, class_count,
     cen_hbm, coef_hbm, bat_hbm, lab_hbm, idx_hbm, sub_hbm, eig_hbm, scale_hbm,
     pred_hbm, new_hbm,
-    batch, cen, eig, sk, xsend, xrecv, acc, zsend, zrecv, pred, eall, upd,
-    coef_ref, lab_ref, idx_ref, sub_ref, eig_ref, scale_ref,
+    batch, cen, eig, sk, sk_own, skq, pick, xsend, xrecv, acc, zsend, zrecv, pred, upd,
+    pred_ref, coef_ref, lab_ref, idx_ref, sub_ref, eig_ref, scale_ref,
     send_sem, recv_sem, local_sem,
 ):
     nz = rows // NX
@@ -182,6 +182,8 @@
     cen_rows = cen_wide.astype(jnp.bfloat16)
 
     later = []
+    pick[...] = pick_t
+    pick_own = pick[eig_rows, :]
 
     def part_pred(first, second):
         both = jnp.concatenate([batch[first], batch[second]], axis=1)
@@ -193,12 +195,9 @@
 
     def subset_part():
         for first, second, high, low in later:
-            sk_high = dot_nn(pick_t, high).astype(jnp.bfloat16)
-            sk_low = dot_nn(pick_t, low).astype(jnp.bfloat16)
+            both = dot_nn(pick_own, high) + dot_nn(pick_own, low)
             for at, row in enumerate((first, second)):
-                lanes = slice(at * cols, (at + 1) * cols)
-                sk[row, 0:subset_count, :] = sk_high[:, lanes]
-                sk[row, subset_count:2 * subset_count, :] = sk_low[:, lanes]
+                sk_own[row] = both[:, at * cols:(at + 1) * cols]
         later.clear()
 
     for i in range(nz - 1, -1, -1):
@@ -219,10 +218,18 @@
         for i in (d, d + 1):
             xy_in[i](slot(far[i], cy))
             far_in[i].append(pass_on(far[i], cy, k_dev))
+    ey_in, ek_in = [], []
+
+    def eig_on(row):
+        ey_in.append((send(eig.at[row, c], eig.at[row, c], y_dev), row))
+        ek_in.append((send(eig.at[row, c], eig.at[row, c], k_dev), row, ck))
+
+    eig_on(r)
     ex_in = [send(own_eig, eig.at[r, c], x_dev)]
     for d in range(1, nz):
         ez_in[d](eig.at[near[d], c])
         ex_in.append(send(eig.at[near[d], c], eig.at[near[d], c], x_dev))
+        eig_on(near[d])
     for d in range(0, nz, 2):
         for i in (d, d + 1):
             far_in[i][0](slot(far[i], ck))
@@ -240,14 +247,24 @@
     total = acc[0] + unpack(xrecv.at[0])
     subset_part()
 
-    ey_in, ek_in = [], []
-
-    def eig_on(row):
-        ey_in.append((send(eig.at[row, c], eig.at[row, c], y_dev), row))
-        ek_in.append((send(eig.at[row, c], eig.at[row, c], k_dev), row, ck))
-
-    for row in near:
-        eig_on(row)
+    values = jnp.concatenate([sk_own[row] for row in range(rows)], axis=1)
+    top = jnp.maximum(jnp.max(values, axis=1, keepdims=True), 1e-37)
+    code = jnp.clip(jnp.ceil(jnp.log2(top) * STEPS) + 1.0, -32000.0, 32000.0)
+    level = jnp.clip(jnp.round(values * (LARGEST * jnp.exp2(-code / STEPS))), -LARGEST, LARGEST)
+    level = level.astype(jnp.int32).astype(jnp.int16)
+    for row in range(rows):
+        skq[r, c, row] = level[:, row * cols:(row + 1) * cols]
+    codes = jnp.broadcast_to(code, (eig_part, cols))
+    skq[r, c, rows] = codes.astype(jnp.int32).astype(jnp.int16)
+
+    def kern_on(row, col, dev):
+        return send(skq.at[row, col], skq.at[row, col], dev)
+
+    kz_in = [None] + [kern_on(r, c, z_dev(d)) for d in range(1, nz)]
+    kx_in = [kern_on(r, c, x_dev)]
+    ky_in = [(kern_on(r, c, y_dev), r)]
+    kk_in = [(kern_on(r, c, k_dev), r, ck)]
+
     for d in range(1, nz):
         rs_in[d](zrecv.at[d - 1])
         total += unpack(zrecv.at[d - 1])
@@ -257,9 +274,45 @@
     pz_in = [None] + [send(pred.at[mine], pred.at[mine], z_dev(d)) for d in range(1, nz)]
     px_in = [send(pred.at[mine], pred.at[mine], x_dev)]
 
+    for d in range(1, nz):
+        kz_in[d](skq.at[near[d], c])
+        kx_in.append(kern_on(near[d], c, x_dev))
+        ky_in.append((kern_on(near[d], c, y_dev), near[d]))
+        kk_in.append((kern_on(near[d], c, k_dev), near[d], ck))
     for arrive, row in zip(ex_in, far):
         arrive(eig.at[row, c])
         eig_on(row)
+    for i in range(1, nz):
+        pz_in[i](pred.at[far[i]])
+        px_in.append(send(pred.at[far[i]], pred.at[far[i]], x_dev))
+    for arrive, row in zip(kx_in, far):
+        arrive(skq.at[row, c])
+        ky_in.append((kern_on(row, c, y_dev), row))
+        kk_in.append((kern_on(row, c, k_dev), row, ck))
+    for arrive, row in ey_in:
+        arrive(eig.at[row, cy])
+        ek_in.append((send(eig.at[row, cy], eig.at[row, cy], k_dev), row, cyk))
+    for arrive, row in ky_in:
+        arrive(skq.at[row, cy])
+        kk_in.append((kern_on(row, cy, k_dev), row, cyk))
+    for arrive, row, col in ek_in:
+        arrive(eig.at[row, col])
+    whole_high, whole_low = split(eig[...].reshape(rows * subset_count, eig_ref.shape[1]))
+    own_high, own_low = split(eig_ref[...] * scale_ref[...])
+    metric = dot_nt(own_high, whole_high) + dot_nt(own_high, whole_low)
+    metric_high, metric_low = split(metric + dot_nt(own_low, whole_high))
+    for arrive, row, col in kk_in:
+        arrive(skq.at[row, col])
+    flat = (rows * subset_count, cols)
+    units = skq[:, :, rows].astype(jnp.int32).astype(jnp.float32).reshape(flat)
+    units = jnp.exp2(units / STEPS) / LARGEST
+    for row in range(rows):
+        levels = skq[:, :, row].astype(jnp.int32).astype(jnp.float32).reshape(flat)
+        high, low = split(levels * units)
+        mixed = dot_nn(metric_high, high) + dot_nn(metric_high, low) + dot_nn(metric_low, high)
+        high, low = split(mixed)
+        sk[row, 0:subset_count, :] = high
+        sk[row, subset_count:2 * subset_count, :] = low
 
     class_ids = lax.broadcasted_iota(jnp.int32, (padded, cols), 0) + c * class_count
     center_ids = lax.broadcasted_iota(jnp.int32, (row_count, cols), 0) + first_row
@@ -272,10 +325,11 @@
             columns = pl.ds(pl.multiple_of(row * cols, cols), cols)
             n = 9 + len(leaving)
             leaving.append(
-                pltpu.make_async_copy(pred.at[row], pred_hbm.at[:, columns], local_sem.at[n])
+                pltpu.make_async_copy(pred_ref.at[row], pred_hbm.at[:, columns], local_sem.at[n])
             )
+            value = unpack(pred.at[row])
+            pred_ref[row] = value[0:class_count]
             leaving[-1].start()
-            value = unpack(pred.at[row])
             grads.append(value - (lab_ref[pl.ds(row, 1), :] == class_ids).astype(jnp.float32))
             kernels.append(sk[row])
         high, low = split(jnp.concatenate(grads, axis=1))
@@ -296,10 +350,6 @@
     error = jnp.zeros((subset_count, padded), jnp.float32)
     update = jnp.zeros((padded, row_count), jnp.float32)
     for d in range(0, nz, 2):
-        for i in (d, d + 1):
-            if i > 0:
-                pz_in[i](pred.at[far[i]])
-                px_in.append(send(pred.at[far[i]], pred.at[far[i]], x_dev))
         error, move = use_pair((far[d], far[d + 1]), error)
         update = scatter(update, [move])
     moves = []
@@ -309,28 +359,8 @@
         error, move = use_pair((near[d], near[d + 1]), error)
         moves.append(move)
 
-    pack(error, eall.at[r])
-    fz_in = [None] + [send(eall.at[r], eall.at[r], z_dev(d)) for d in range(1, nz)]
-    fx_in = [send(eall.at[r], eall.at[r], x_dev)]
-    for arrive, row in ey_in:
-        arrive(eig.at[row, cy])
-        ek_in.append((send(eig.at[row, cy], eig.at[row, cy], k_dev), row, cyk))
-    upd[...] = coef - step_rate * scatter(update, moves[:1])
-    for d in range(1, nz):
-        fz_in[d](eall.at[near[d]])
-        fx_in.append(send(eall.at[near[d]], eall.at[near[d]], x_dev))
-    upd[...] -= step_rate * scatter(jnp.zeros_like(update), moves[1:])
-    for arrive, row, col in ek_in:
-        arrive(eig.at[row, col])
-    whole_high, whole_low = split(eig[...].reshape(rows * subset_count, eig_ref.shape[1]))
-    own_high, own_low = split(eig_ref[...] * scale_ref[...])
-    metric = dot_nt(own_high, whole_high) + dot_nt(own_high, whole_low)
-    metric_high, metric_low = split(metric + dot_nt(own_low, whole_high))
-    for d in range(nz):
-        fx_in[d](eall.at[far[d]])
-    high, low = split(jnp.concatenate([unpack(eall.at[row]) for row in range(rows)], axis=0))
-    correction = dot_nn(metric_high, high) + dot_nn(metric_high, low) + dot_nn(metric_low, high)
-    high, low = split(jnp.transpose(correction))
+    upd[...] = coef - step_rate * scatter(update, moves)
+    high, low = split(jnp.transpose(error))
     moved = dot_nn(high, pick_t) + dot_nn(low, pick_t)
     coef_ref[...] = (upd[...] + step_rate * moved)[0:class_count]
     leaving.append(pltpu.make_async_copy(coef_ref, new_hbm, local_sem.at[9 + rows]))
@@ -352,13 +382,13 @@
     subset_count, eig_count = eigen_vectors.shape
     padded = -(-class_count // 16) * 16
     nz = rows // NX
-    copies = 13 * rows + 40
+    copies = 16 * rows + 40
     f32, short = jnp.float32, jnp.int16
     hbm = pl.BlockSpec(memory_space=pltpu.HBM)
-    levels, updated = pl.pallas_call(
+    return pl.pallas_call(
         functools.partial(fused_kernel, rows, cls, class_count),
         out_shape=(
-            jax.ShapeDtypeStruct((padded + 16, rows * cols), short),
+            jax.ShapeDtypeStruct((class_count, rows * cols), f32),
             jax.ShapeDtypeStruct((class_count, row_count), f32),
         ),
         in_specs=[hbm] * 8,
@@ -368,14 +398,17 @@
             pltpu.VMEM((cls * width, row_count), jnp.bfloat16),
             pltpu.VMEM((rows, cls, subset_count // cls, eig_count), f32),
             pltpu.VMEM((rows, 2 * subset_count, cols), jnp.bfloat16),
+            pltpu.VMEM((rows, subset_count // cls, cols), f32),
+            pltpu.VMEM((rows, cls, rows + 1, subset_count // cls, cols), short),
+            pltpu.VMEM((subset_count, row_count), jnp.bfloat16),
             pltpu.VMEM((nz, padded + 16, cols), short),
             pltpu.VMEM((nz, padded + 16, cols), short),
             pltpu.VMEM((nz, padded, cols), f32),
             pltpu.VMEM((nz - 1, padded + 16, cols), short),
             pltpu.VMEM((nz - 1, padded + 16, cols), short),
             pltpu.VMEM((rows, padded + 16, cols), short),
-            pltpu.VMEM((rows, subset_count + 16, padded), short),
             pltpu.VMEM((padded, row_count), f32),
+            pltpu.VMEM((rows, class_count, cols), f32),
             pltpu.VMEM((class_count, row_count), f32),
             pltpu.VMEM((rows, cols), jnp.int32),
             pltpu.VMEM((rows, cols), jnp.int32),
@@ -395,8 +428,6 @@
         subset_index.reshape(1, subset_count), eigen_vectors,
         eigen_scale.reshape(1, eig_count),
     )
-    unit = jnp.exp2(levels[padded:padded + 1].astype(f32) / STEPS) / LARGEST
-    return levels[0:class_count].astype(f32) * unit, updated
 
 
 def plain_shards(

time: 61.7 us -> 59.5 us (0.964)
  other arithmetic: 2.98 us -> 0 us
  local copies, waits for them, and re-layouts: 0.71 us -> 3.06 us
  Pallas kernels: 57.1 us -> 55.5 us
    unnamed x3 -> x4, local copies, waits for them, and re-layouts: 0.71 us -> 3.06 us
    mul x1 -> x0, other arithmetic: 2.24 us -> none  [fused_shards(): return (levels[0:class_count].astype(f32) * unit, updated)]
    pallas_call x1, Pallas kernels: 57.1 us -> 55.5 us  [fused_shards(): pl.pallas_call(functools.partial(fused_kernel, rows, cls, class_count), o...]
    div x1 -> x0, other arithmetic: 0.74 us -> none  [fused_shards(): unit = jnp.exp2(levels[padded:padded + 1].astype(f32) / STEPS) / LARGEST]
where the time goes in v6:
time: 59.5 us; the launch traced here: 59.2 us
  Pallas kernels  55.5 us (93%)
  local copies, waits for them, and re-layouts  3.06 us (5%)
  between operations  0.65 us (1%)
    pallas_call x1, Pallas kernels, fused_shards(): pl.pallas_call(functools.partial(fused_kernel, rows, cls, class_count), o...  55.5 us
    unnamed x4, local copies, waits for them, and re-layouts  3.06 us

profile of v6, /device:TPU:0, one launch (start us, length us, event | category | flops | bytes accessed | tf_op | source)
XLA Modules:
  0.0 59.2 jit_solution(12064149007293709520)
XLA Ops:
  0.6 55.5 %shard_map.95 = (f32[250,1024]{1,0:T(8,128)}, f32[250,256]{1,0:T(8,128)}) custom-call(bf16[320,256]{1,0:T(8,128)(2,1)} %bitcast.6, f32[250,256]{1,0:T(8,128)} %coef_hbm.1, bf16[320,128]{1,0:T(8,128)(2,1)} %bitcast.7, s32[8,128]{1,0:T(8,128)} %bitcast.8, s32[8,128]{1,0:T(8,128)} %bitcast.9, s32[1,64]{1,0:T(1,128)} %bitcast.11, f32[64,512]{1,0:T(8,128)} %eig_hbm.1, ...), custom_call_target="tpu_custom_call" | custom-call | tf_op jit(solution)/shard_map/pallas_call | solution.py:388
  56.1 0.0 copy-start
  56.1 2.3 %copy.12 = f32[250,1024]{1,0:T(8,128)} copy(f32[250,1024]{1,0:T(8,128)} %get-tuple-element.4) | data formatting | bytes 2048000
  58.5 0.0 copy-done
  58.5 0.7 %copy.13 = f32[250,256]{1,0:T(8,128)} copy(f32[250,256]{1,0:T(8,128)S(1)} %copy-done) | data formatting | bytes 512000
Async XLA Ops:
  56.1 2.4 %copy-start = (f32[250,256]{1,0:T(8,128)S(1)}, f32[250,256]{1,0:T(8,128)}, u32[]{:S(2)}) copy-start(f32[250,256]{1,0:T(8,128)} %get-tuple-element.5) | copy-start | bytes 768004

commit v7 on v6

--- a/solution.py
+++ b/solution.py
@@ -279,12 +279,12 @@
         kx_in.append(kern_on(near[d], c, x_dev))
         ky_in.append((kern_on(near[d], c, y_dev), near[d]))
         kk_in.append((kern_on(near[d], c, k_dev), near[d], ck))
+    for i in range(1, nz):
+        pz_in[i](pred.at[far[i]])
+        px_in.append(send(pred.at[far[i]], pred.at[far[i]], x_dev))
     for arrive, row in zip(ex_in, far):
         arrive(eig.at[row, c])
         eig_on(row)
-    for i in range(1, nz):
-        pz_in[i](pred.at[far[i]])
-        px_in.append(send(pred.at[far[i]], pred.at[far[i]], x_dev))
     for arrive, row in zip(kx_in, far):
         arrive(skq.at[row, c])
         ky_in.append((kern_on(row, c, y_dev), row))
@@ -306,13 +306,23 @@
     flat = (rows * subset_count, cols)
     units = skq[:, :, rows].astype(jnp.int32).astype(jnp.float32).reshape(flat)
     units = jnp.exp2(units / STEPS) / LARGEST
-    for row in range(rows):
-        levels = skq[:, :, row].astype(jnp.int32).astype(jnp.float32).reshape(flat)
-        high, low = split(levels * units)
-        mixed = dot_nn(metric_high, high) + dot_nn(metric_high, low) + dot_nn(metric_low, high)
+    metric_both = jnp.concatenate([metric_high, metric_low], axis=0)
+    for first in range(0, rows, 2):
+        values = jnp.concatenate(
+            [
+                skq[:, :, row].astype(jnp.int32).astype(jnp.float32).reshape(flat) * units
+                for row in (first, first + 1)
+            ],
+            axis=1,
+        )
+        high, low = split(values)
+        two = dot_nn(metric_both, high)
+        mixed = two[0:subset_count] + two[subset_count:] + dot_nn(metric_high, low)
         high, low = split(mixed)
-        sk[row, 0:subset_count, :] = high
-        sk[row, subset_count:2 * subset_count, :] = low
+        for at in range(2):
+            lanes = slice(at * cols, (at + 1) * cols)
+            sk[first + at, 0:subset_count, :] = high[:, lanes]
+            sk[first + at, subset_count:2 * subset_count, :] = low[:, lanes]
 
     class_ids = lax.broadcasted_iota(jnp.int32, (padded, cols), 0) + c * class_count
     center_ids = lax.broadcasted_iota(jnp.int32, (row_count, cols), 0) + first_row

time: 59.5 us -> 60.6 us (1.018)
  Pallas kernels: 55.5 us -> 56.6 us
    pallas_call x1, Pallas kernels: 55.5 us -> 56.6 us  [fused_shards(): pl.pallas_call(functools.partial(fused_kernel, rows, cls, class_count), o...]
where the time goes in v7:
time: 60.6 us; the launch traced here: 60.3 us
  Pallas kernels  56.6 us (93%)
  local copies, waits for them, and re-layouts  3.06 us (5%)
  between operations  0.65 us (1%)
    pallas_call x1, Pallas kernels, fused_shards(): pl.pallas_call(functools.partial(fused_kernel, rows, cls, class_count), o...  56.6 us
    unnamed x4, local copies, waits for them, and re-layouts  3.06 us

profile of v7, /device:TPU:0, one launch (start us, length us, event | category | flops | bytes accessed | tf_op | source)
XLA Modules:
  0.0 60.3 jit_solution(3415534079481108811)
XLA Ops:
  0.6 56.6 %shard_map.95 = (f32[250,1024]{1,0:T(8,128)}, f32[250,256]{1,0:T(8,128)}) custom-call(bf16[320,256]{1,0:T(8,128)(2,1)} %bitcast.6, f32[250,256]{1,0:T(8,128)} %coef_hbm.1, bf16[320,128]{1,0:T(8,128)(2,1)} %bitcast.7, s32[8,128]{1,0:T(8,128)} %bitcast.8, s32[8,128]{1,0:T(8,128)} %bitcast.9, s32[1,64]{1,0:T(1,128)} %bitcast.11, f32[64,512]{1,0:T(8,128)} %eig_hbm.1, ...), custom_call_target="tpu_custom_call" | custom-call | tf_op jit(solution)/shard_map/pallas_call | solution.py:398
  57.3 0.0 copy-start
  57.3 2.3 %copy.12 = f32[250,1024]{1,0:T(8,128)} copy(f32[250,1024]{1,0:T(8,128)} %get-tuple-element.4) | data formatting | bytes 2048000
  59.6 0.0 copy-done
  59.6 0.7 %copy.13 = f32[250,256]{1,0:T(8,128)} copy(f32[250,256]{1,0:T(8,128)S(1)} %copy-done) | data formatting | bytes 512000
Async XLA Ops:
  57.3 2.4 %copy-start = (f32[250,256]{1,0:T(8,128)S(1)}, f32[250,256]{1,0:T(8,128)}, u32[]{:S(2)}) copy-start(f32[250,256]{1,0:T(8,128)} %get-tuple-element.5) | copy-start | bytes 768004

commit v8 on v7

--- a/solution.py
+++ b/solution.py
@@ -279,12 +279,12 @@
         kx_in.append(kern_on(near[d], c, x_dev))
         ky_in.append((kern_on(near[d], c, y_dev), near[d]))
         kk_in.append((kern_on(near[d], c, k_dev), near[d], ck))
+    for arrive, row in zip(ex_in, far):
+        arrive(eig.at[row, c])
+        eig_on(row)
     for i in range(1, nz):
         pz_in[i](pred.at[far[i]])
         px_in.append(send(pred.at[far[i]], pred.at[far[i]], x_dev))
-    for arrive, row in zip(ex_in, far):
-        arrive(eig.at[row, c])
-        eig_on(row)
     for arrive, row in zip(kx_in, far):
         arrive(skq.at[row, c])
         ky_in.append((kern_on(row, c, y_dev), row))

time: 60.6 us -> 59.3 us (0.979)
  Pallas kernels: 56.6 us -> 55.4 us
    pallas_call x1, Pallas kernels: 56.6 us -> 55.4 us  [fused_shards(): pl.pallas_call(functools.partial(fused_kernel, rows, cls, class_count), o...]
where the time goes in v8:
time: 59.3 us; the launch traced here: 59.1 us
  Pallas kernels  55.4 us (93%)
  local copies, waits for them, and re-layouts  3.06 us (5%)
  between operations  0.65 us (1%)
    pallas_call x1, Pallas kernels, fused_shards(): pl.pallas_call(functools.partial(fused_kernel, rows, cls, class_count), o...  55.4 us
    unnamed x4, local copies, waits for them, and re-layouts  3.06 us

profile of v8, /device:TPU:0, one launch (start us, length us, event | category | flops | bytes accessed | tf_op | source)
XLA Modules:
  0.0 59.1 jit_solution(17377723880386847014)
XLA Ops:
  0.6 55.4 %shard_map.95 = (f32[250,1024]{1,0:T(8,128)}, f32[250,256]{1,0:T(8,128)}) custom-call(bf16[320,256]{1,0:T(8,128)(2,1)} %bitcast.6, f32[250,256]{1,0:T(8,128)} %coef_hbm.1, bf16[320,128]{1,0:T(8,128)(2,1)} %bitcast.7, s32[8,128]{1,0:T(8,128)} %bitcast.8, s32[8,128]{1,0:T(8,128)} %bitcast.9, s32[1,64]{1,0:T(1,128)} %bitcast.11, f32[64,512]{1,0:T(8,128)} %eig_hbm.1, ...), custom_call_target="tpu_custom_call" | custom-call | tf_op jit(solution)/shard_map/pallas_call | solution.py:398
  56.0 0.0 copy-start
  56.0 2.3 %copy.12 = f32[250,1024]{1,0:T(8,128)} copy(f32[250,1024]{1,0:T(8,128)} %get-tuple-element.4) | data formatting | bytes 2048000
  58.4 0.0 copy-done
  58.4 0.7 %copy.13 = f32[250,256]{1,0:T(8,128)} copy(f32[250,256]{1,0:T(8,128)S(1)} %copy-done) | data formatting | bytes 512000
Async XLA Ops:
  56.0 2.4 %copy-start = (f32[250,256]{1,0:T(8,128)S(1)}, f32[250,256]{1,0:T(8,128)}, u32[]{:S(2)}) copy-start(f32[250,256]{1,0:T(8,128)} %get-tuple-element.5) | copy-start | bytes 768004
